TPU v7x, 32 devices: a whole 2x2x4 slice. The times are simulated.
32 devices in a mesh: blk: 16 (over z, x, core), head: 2 (over y).
Axes of the slice: x: 2, y: 2, z: 4, core: 2. Of those that a mesh axis runs over, the one named last changes fastest.
Arguments:
- token_ids: int32 [4096], P('blk'), may hold values from 0 to 32127
- targets: int32 [4096], P('blk'), may hold values from 0 to 32127
- valid_mask: int32 [4096], replicated, may hold values from 0 to 1
- cont_lengths: int32 [16], replicated, may hold values from 1 to 256, 2048 in all
- routes: int32 [2, 4096], P(None, 'blk'), may hold values from 0 to 1
- vocab_table: float32 [32128, 768], P(('blk', 'head')), may hold values from -12 to 12
- vocab_first: float32 [32128, 768], P(('blk', 'head')), may hold values from -2.3841858e-06 to 2.3841858e-06
- vocab_second: float32 [32128, 768], P(('blk', 'head')), may hold values from 1.03575046e-13 to 4.1430019e-13
- attn_weights: float32 [2, 768, 3072], P(None, ('blk', 'head')), may hold values from -2.309401 to 2.309401
- attn_first: float32 [2, 768, 3072], P(None, ('blk', 'head')), may hold values from -2.3841858e-06 to 2.3841858e-06
- attn_second: float32 [2, 768, 3072], P(None, ('blk', 'head')), may hold values from 1.03575046e-13 to 4.1430019e-13
- router: float32 [2, 768, 2], P(None, ('blk', 'head')), may hold values from -0.375 to 0.375
- router_first: float32 [2, 768, 2], P(None, ('blk', 'head')), may hold values from -2.3841858e-06 to 2.3841858e-06
- router_second: float32 [2, 768, 2], P(None, ('blk', 'head')), may hold values from 1.03575046e-13 to 4.1430019e-13
- norm_gains: float32 [5, 768], P(None, ('blk', 'head')), may hold values from 0.25 to 2.2
- gains_first: float32 [5, 768], P(None, ('blk', 'head')), may hold values from -6.1035156e-05 to 6.1035156e-05
- gains_second: float32 [5, 768], P(None, ('blk', 'head')), may hold values from 9.3217545e-11 to 3.7287018e-10
- expert_up: float32 [2, 2, 768, 3072], P(None, None, 'blk', 'head'), may hold values from -0.21875 to 0.21875
- up_first: float32 [2, 2, 768, 3072], P(None, None, 'blk', 'head'), may hold values from -2.3841858e-06 to 2.3841858e-06
- up_second: float32 [2, 2, 768, 3072], P(None, None, 'blk', 'head'), may hold values from 1.03575046e-13 to 4.1430019e-13
- expert_down: float32 [2, 2, 768, 3072], P(None, None, 'blk', 'head'), may hold values from -0.21875 to 0.21875
- down_first: float32 [2, 2, 768, 3072], P(None, None, 'blk', 'head'), may hold values from -2.3841858e-06 to 2.3841858e-06
- down_second: float32 [2, 2, 768, 3072], P(None, None, 'blk', 'head'), may hold values from 1.03575046e-13 to 4.1430019e-13
Outputs:
- loss_sum: float32 [], replicated
- token_count: float32 [], replicated
- grad_norm: float32 [], replicated
- vocab_out: float32 [32128, 768], P(('blk', 'head'))
- vocab_first_out: float32 [32128, 768], P(('blk', 'head'))
- vocab_second_out: float32 [32128, 768], P(('blk', 'head'))
- attn_out: float32 [2, 768, 3072], P(None, ('blk', 'head'))
- attn_first_out: float32 [2, 768, 3072], P(None, ('blk', 'head'))
- attn_second_out: float32 [2, 768, 3072], P(None, ('blk', 'head'))
- router_out: float32 [2, 768, 2], P(None, ('blk', 'head'))
- router_first_out: float32 [2, 768, 2], P(None, ('blk', 'head'))
- router_second_out: float32 [2, 768, 2], P(None, ('blk', 'head'))
- gains_out: float32 [5, 768], P(None, ('blk', 'head'))
- gains_first_out: float32 [5, 768], P(None, ('blk', 'head'))
- gains_second_out: float32 [5, 768], P(None, ('blk', 'head'))
- up_out: float32 [2, 2, 768, 3072], P(None, None, 'blk', 'head')
- up_first_out: float32 [2, 2, 768, 3072], P(None, None, 'blk', 'head')
- up_second_out: float32 [2, 2, 768, 3072], P(None, None, 'blk', 'head')
- down_out: float32 [2, 2, 768, 3072], P(None, None, 'blk', 'head')
- down_first_out: float32 [2, 2, 768, 3072], P(None, None, 'blk', 'head')
- down_second_out: float32 [2, 2, 768, 3072], P(None, None, 'blk', 'head')
Inputs may be any that keep to these rules, and one draw needn't show every extreme that they name: `cont_lengths`: continuation j covers the positions that follow the prompt and the continuations before it.
All inputs are finite; a program needn't handle non-finite values.
Results may differ from a plain program's by a relative error of at most 0.013.
Values may be sent and summed in bfloat16 or wider, within the bound.
A program may use at most 448 MiB of HBM per device.

v0:
```python
import functools

import jax
import jax.numpy as jnp
from jax import lax
from jax.experimental import pallas as pl
from jax.experimental.pallas import tpu as pltpu
from jax.sharding import Mesh, PartitionSpec as P

D = 768
HEADS = 12
HEAD_DIM = 64
EXPERTS = 2
LAYERS = 2
PROMPT = 2048
STEP = 10

NORM_EPS = 1e-06
BETA_ONE = 0.9
BETA_TWO = 0.95
ADAM_EPS = 1e-08
CLIP_AT = 0.01
MASKED = -1e30
STEP_RATES = (2.0, 0.25, 0.04, 0.4, 0.04, 0.04)
DECAY_RATES = (0.01, 0.01, 0.01, 0.0, 0.01, 0.01)

ALL = ("z", "x", "core", "head")
BLK = ("z", "x", "core")
PLANE = ("x", "head")
LINE = ("z", "core")
MIB = 2**20
MESH = pl.DeviceIdType.MESH
ANY = pl.BlockSpec(memory_space=pl.ANY)
VMEM = pl.BlockSpec(memory_space=pltpu.VMEM)
HBM = pl.BlockSpec(memory_space=pltpu.HBM)


def rms_norm(stream, gain):
    return stream * lax.rsqrt(jnp.mean(stream * stream, axis=-1, keepdims=True) + NORM_EPS) * gain


def segment_of(position, cont_ends):
    later = jnp.sum((cont_ends[None, :] <= (position - PROMPT)[:, None]).astype(jnp.int32), axis=1)
    return jnp.where(position < PROMPT, 0, 1 + later)


def place():
    return tuple(lax.axis_index(name) for name in ALL)


def sizes():
    return tuple(lax.axis_size(name) for name in ALL)


def remote(source, target, send, receive, device):
    return pltpu.make_async_remote_copy(
        src_ref=source, dst_ref=target, send_sem=send, recv_sem=receive,
        device_id=device, device_id_type=MESH,
    )


def greet(devices):
    barrier = pltpu.get_barrier_semaphore()
    for device in devices:
        pl.semaphore_signal(barrier, inc=1, device_id=device, device_id_type=MESH)
    pl.semaphore_wait(barrier, len(devices))


def around():
    z, x, c, y = place()
    return (z, x, c, y), (z, 1 - x, c, y), (z, x, c, 1 - y), (z, x, 1 - c, y)


def swap_kernel(broadcast, source, out, send_sem, receive_sem, own_sem):
    n_z, n_x, n_c, n_y = sizes()
    count = n_z * n_x * n_c * n_y
    z, x, c, y = place()
    me = ((z * n_x + x) * n_c + c) * n_y + y

    def device_of(index):
        return (
            index // (n_x * n_c * n_y), index // (n_c * n_y) % n_x, index // n_y % n_c, index % n_y
        )

    def taken(index):
        return source.at[0] if broadcast else source.at[index]

    barrier = pltpu.get_barrier_semaphore()

    def call(step, unused):
        other = lax.rem(me + step, count)
        pl.semaphore_signal(barrier, inc=1, device_id=device_of(other), device_id_type=MESH)
        return unused

    lax.fori_loop(1, count, call, 0)
    own = pltpu.make_async_copy(taken(me), out.at[me], own_sem)
    own.start()
    pl.semaphore_wait(barrier, count - 1)

    def copy(step):
        other = lax.rem(me + step, count)
        return remote(
            taken(other), out.at[me], send_sem.at[step], receive_sem.at[step], device_of(other)
        )

    def start(step, unused):
        copy(step).start()
        return unused

    def finish(step, unused):
        copy(step).wait()
        return unused

    lax.fori_loop(1, count, start, 0)
    lax.fori_loop(1, count, finish, 0)
    own.wait()


def swap(blocks, broadcast, collective_id):
    count = 1
    for size in sizes():
        count *= size
    return pl.pallas_call(
        functools.partial(swap_kernel, broadcast),
        out_shape=jax.ShapeDtypeStruct((count,) + blocks.shape[1:], blocks.dtype),
        in_specs=[VMEM],
        out_specs=VMEM,
        scratch_shapes=[
            pltpu.SemaphoreType.DMA((count,)),
            pltpu.SemaphoreType.DMA((count,)),
            pltpu.SemaphoreType.DMA,
        ],
        cost_estimate=pl.CostEstimate(
            flops=0, bytes_accessed=36 * MIB, transcendentals=0
        ),
        compiler_params=pltpu.CompilerParams(
            collective_id=collective_id, has_side_effects=True, vmem_limit_bytes=8 * MIB
        ),
    )(blocks)


def total_of(*parts):
    total = parts[0].astype(jnp.float32)
    for part in parts[1:]:
        total = total + part.astype(jnp.float32)
    return total


PIECES = 4


def spread_kernel(
    prompt_slabs, own_rows, far, near, tail, z_send, z_recv, c_send, c_recv, n_send, n_recv, own_sem
):
    n_z = lax.axis_size("z")
    lane = own_rows.shape[0]
    chunk = lane // 2
    size = lane // PIECES
    (z, x, c, y), _, _, c_near = around()
    above, below = (z + 1, x, c, y), (z - 1, x, c, y)
    in_prompt = z < prompt_slabs
    takes_down = z < prompt_slabs - 1
    gives_down = (z > 0) & (z < prompt_slabs)

    barrier = pltpu.get_barrier_semaphore()
    pl.semaphore_signal(barrier, inc=1, device_id=c_near, device_id_type=MESH)

    @pl.when(z > 0)
    def _():
        pl.semaphore_signal(barrier, inc=1, device_id=below, device_id_type=MESH)

    @pl.when(takes_down)
    def _():
        pl.semaphore_signal(barrier, inc=1, device_id=above, device_id_type=MESH)

    first, second = pl.ds(0, chunk), pl.ds(chunk, chunk)
    own = [
        pltpu.make_async_copy(own_rows.at[first], near.at[1], own_sem.at[0]),
        pltpu.make_async_copy(own_rows.at[second], near.at[3], own_sem.at[1]),
    ]
    own_far = pltpu.make_async_copy(own_rows, far.at[jnp.minimum(z, prompt_slabs - 1), c], own_sem.at[2])
    own_edge = pltpu.make_async_copy(own_rows.at[first], near.at[0], own_sem.at[3])
    edge = (z == 0) & (c == 0)
    for copy in own:
        copy.start()

    @pl.when(in_prompt)
    def _():
        own_far.start()

    @pl.when(edge)
    def _():
        own_edge.start()

    pl.semaphore_wait(
        barrier, 1 + jnp.where(z < n_z - 1, 1, 0) + jnp.where(gives_down, 1, 0)
    )

    def part(index):
        return pl.ds(index * size, size)

    def z_copy(source, slab, index, up):
        return remote(
            source, far.at[slab, c, part(index)], z_send.at[slab, index, 1 if up else 0],
            z_recv.at[slab, index], above if up else below,
        )

    def c_copy(source, slab, index):
        return remote(
            source, far.at[slab, c, part(index)], c_send.at[slab, index], c_recv.at[slab, index], c_near
        )

    def t_copy():
        return remote(own_rows.at[second], tail, n_send.at[0], n_recv.at[0], above)

    def t_hand():
        return remote(tail, near.at[0], n_send.at[1], n_recv.at[1], c_near)

    def n_copy(half):
        slot = jnp.where(c == 0, 2 * half, 2)
        return remote(
            own_rows.at[pl.ds(half * chunk, chunk)], near.at[slot], n_send.at[2 + half], n_recv.at[2 + half],
            c_near,
        )

    @pl.when(in_prompt)
    def _():
        for index in range(PIECES):
            source = own_rows.at[part(index)]

            @pl.when(z < n_z - 1)
            def _():
                z_copy(source, z, index, True).start()

            @pl.when(z > 0)
            def _():
                z_copy(source, z, index, False).start()

            c_copy(source, z, index).start()

    @pl.when((c == 1) & (z < n_z - 1))
    def _():
        t_copy().start()

    n_copy(0).start()

    @pl.when(c == 0)
    def _():
        n_copy(1).start()

    for distance in range(1, n_z):
        low_slab, high_slab = z - distance, z + distance
        for index in range(PIECES):

            @pl.when((low_slab >= 0) & (low_slab < prompt_slabs))
            def _():
                source = far.at[low_slab, c, part(index)]
                z_copy(source, low_slab, index, True).wait_recv()

                @pl.when(z < n_z - 1)
                def _():
                    z_copy(source, low_slab, index, True).start()

                c_copy(source, low_slab, index).start()

            if distance < prompt_slabs:

                @pl.when(high_slab < prompt_slabs)
                def _():
                    source = far.at[high_slab, c, part(index)]
                    z_copy(source, high_slab, index, False).wait_recv()

                    @pl.when(z > 0)
                    def _():
                        z_copy(source, high_slab, index, False).start()

                    c_copy(source, high_slab, index).start()

    @pl.when((c == 1) & (z > 0))
    def _():
        t_copy().wait_recv()
        t_hand().start()
        t_hand().wait_send()

    @pl.when((c == 1) & (z < n_z - 1))
    def _():
        t_copy().wait_send()

    @pl.when((c == 0) & (z > 0))
    def _():
        t_hand().wait_recv()

    n_copy(0).wait_send()
    n_copy(0).wait_recv()

    @pl.when(c == 0)
    def _():
        n_copy(1).wait_send()

    @pl.when(c == 1)
    def _():
        n_copy(1).wait_recv()

    for slab in range(prompt_slabs):
        for index in range(PIECES):
            copy = c_copy(own_rows.at[part(index)], slab, index)
            copy.wait_send()
            copy.wait_recv()

            @pl.when((z < n_z - 1) & (slab <= z))
            def _():
                z_copy(own_rows.at[part(index)], slab, index, True).wait_send()

            @pl.when((z > 0) & (slab >= z))
            def _():
                z_copy(own_rows.at[part(index)], slab, index, False).wait_send()

    for copy in own:
        copy.wait()

    @pl.when(in_prompt)
    def _():
        own_far.wait()

    @pl.when(edge)
    def _():
        own_edge.wait()


def spread_keys(own_rows, prompt_rows, collective_id):
    lane, width = own_rows.shape
    slabs = prompt_rows // (2 * lane)
    dma = pltpu.SemaphoreType.DMA
    far, near, _ = pl.pallas_call(
        functools.partial(spread_kernel, slabs),
        out_shape=(
            jax.ShapeDtypeStruct((slabs, 2, lane, width), own_rows.dtype),
            jax.ShapeDtypeStruct((4, lane // 2, width), own_rows.dtype),
            jax.ShapeDtypeStruct((lane // 2, width), own_rows.dtype),
        ),
        in_specs=[VMEM],
        out_specs=(VMEM,) * 3,
        scratch_shapes=[
            dma((slabs, PIECES, 2)), dma((slabs, PIECES)), dma((slabs, PIECES)), dma((slabs, PIECES)),
            dma((4,)), dma((4,)), dma((4,)),
        ],
        cost_estimate=pl.CostEstimate(
            flops=0, bytes_accessed=60 * MIB, transcendentals=0
        ),
        compiler_params=pltpu.CompilerParams(
            collective_id=collective_id, has_side_effects=True, vmem_limit_bytes=12 * MIB
        ),
    )(own_rows)
    return far.reshape(prompt_rows, width), near.reshape(2 * lane, width)


def collect_kernel(
    prompt_slabs, far, near, query_grad, whole, out, own, c_got, z_got, n_got, tail_pass, tail_got,
    c_send, c_recv, z_send, z_recv, n_send, n_recv,
):
    n_z = lax.axis_size("z")
    lane = out.shape[0]
    chunk = lane // 2
    size = lane // PIECES
    (z, x, c, y), _, _, c_near = around()
    above, below = (z + 1, x, c, y), (z - 1, x, c, y)

    barrier = pltpu.get_barrier_semaphore()
    pl.semaphore_signal(barrier, inc=1, device_id=c_near, device_id_type=MESH)

    @pl.when(z < n_z - 1)
    def _():
        pl.semaphore_signal(barrier, inc=1, device_id=above, device_id_type=MESH)

    pl.semaphore_wait(barrier, 1 + jnp.where(z > 0, 1, 0))

    def part(index):
        return pl.ds(index * size, size)

    def c_copy(slab, index):
        return remote(
            far.at[slab, 1 - c, part(index)], c_got.at[slab, part(index)], c_send.at[slab, index],
            c_recv.at[slab, index], c_near,
        )

    def z_copy(slab, index):
        return remote(
            own.at[slab, part(index)], z_got.at[slab, part(index)], z_send.at[slab, index],
            z_recv.at[slab, index], below,
        )

    def n_copy(half):
        slot = jnp.where(c == 0, 2, 2 * half)
        return remote(near.at[slot], n_got.at[half], n_send.at[half], n_recv.at[half], c_near)

    def t_hand():
        return remote(near.at[0], tail_pass, n_send.at[2], n_recv.at[2], c_near)

    def t_copy():
        return remote(tail_pass, tail_got, n_send.at[3], n_recv.at[3], below)

    for slab in range(prompt_slabs):
        for index in range(PIECES):
            c_copy(slab, index).start()
    n_copy(0).start()

    @pl.when(c == 1)
    def _():
        n_copy(1).start()

    @pl.when((c == 0) & (z > 0))
    def _():
        t_hand().start()

    for slab in range(prompt_slabs):
        for index in range(PIECES):
            c_copy(slab, index).wait_recv()
            rows = part(index)
            mine = total_of(far[slab, c, rows, :], c_got[slab, rows, :])

            @pl.when((z == n_z - 1) & (z > slab))
            def _():
                own[slab, rows, :] = mine.astype(jnp.bfloat16)
                z_copy(slab, index).start()

            @pl.when((z < n_z - 1) & (z > slab))
            def _():
                z_copy(slab, index).wait_recv()
                own[slab, rows, :] = total_of(mine, z_got[slab, rows, :]).astype(jnp.bfloat16)
                z_copy(slab, index).start()

            @pl.when((z < n_z - 1) & (z == slab))
            def _():
                z_copy(slab, index).wait_recv()
                out[rows, :] = total_of(mine, z_got[slab, rows, :])

            @pl.when((z == n_z - 1) & (z == slab))
            def _():
                out[rows, :] = mine

    @pl.when((c == 1) & (z > 0))
    def _():
        t_hand().wait_recv()
        t_copy().start()

    @pl.when(z >= prompt_slabs)
    def _():
        out[...] = jnp.zeros_like(out)

    n_copy(0).wait_recv()
    first, second = pl.ds(0, chunk), pl.ds(chunk, chunk)
    out[first, :] += total_of(near[1], n_got[0])
    out[second, :] += near[3].astype(jnp.float32)

    @pl.when(c == 0)
    def _():
        n_copy(1).wait_recv()
        out[second, :] += n_got[1].astype(jnp.float32)

    @pl.when((c == 1) & (z < n_z - 1))
    def _():
        t_copy().wait_recv()
        out[second, :] += tail_got[...].astype(jnp.float32)

    whole[...] = jnp.concatenate([out[...].astype(jnp.bfloat16), query_grad[...]], axis=1)

    @pl.when((c == 1) & (z > 0))
    def _():
        t_copy().wait_send()

    @pl.when((c == 0) & (z > 0))
    def _():
        t_hand().wait_send()

    n_copy(0).wait_send()

    @pl.when(c == 1)
    def _():
        n_copy(1).wait_send()

    for slab in range(prompt_slabs):
        for index in range(PIECES):
            c_copy(slab, index).wait_send()

            @pl.when(z > slab)
            def _():
                z_copy(slab, index).wait_send()


def collect_keys(far, near, query_grad, collective_id):
    prompt_rows, width = far.shape
    lane = near.shape[0] // 2
    slabs = prompt_rows // (2 * lane)
    dma = pltpu.SemaphoreType.DMA
    low = jnp.bfloat16
    return pl.pallas_call(
        functools.partial(collect_kernel, slabs),
        out_shape=jax.ShapeDtypeStruct((lane, width + query_grad.shape[1]), low),
        in_specs=[VMEM] * 3,
        out_specs=VMEM,
        scratch_shapes=[
            pltpu.VMEM((lane, width), jnp.float32),
            pltpu.VMEM((slabs, lane, width), low),
            pltpu.VMEM((slabs, lane, width), low),
            pltpu.VMEM((slabs, lane, width), low),
            pltpu.VMEM((2, lane // 2, width), low),
            pltpu.VMEM((lane // 2, width), low),
            pltpu.VMEM((lane // 2, width), low),
            dma((slabs, PIECES)), dma((slabs, PIECES)), dma((slabs, PIECES)), dma((slabs, PIECES)),
            dma((4,)), dma((4,)),
        ],
        cost_estimate=pl.CostEstimate(
            flops=0, bytes_accessed=60 * MIB, transcendentals=0
        ),
        compiler_params=pltpu.CompilerParams(
            collective_id=collective_id, has_side_effects=True, vmem_limit_bytes=20 * MIB
        ),
    )(far.astype(low).reshape(slabs, 2, lane, width), near.astype(low).reshape(4, lane // 2, width), query_grad)


def greet_all():
    n_z, n_x, n_c, n_y = sizes()
    count = n_z * n_x * n_c * n_y
    barrier = pltpu.get_barrier_semaphore()

    def call(step, unused):
        pl.semaphore_signal(barrier, inc=1, device_id=device_after(step), device_id_type=MESH)
        return unused

    lax.fori_loop(1, count, call, 0)
    pl.semaphore_wait(barrier, count - 1)


def index_after(step):
    n_z, n_x, n_c, n_y = sizes()
    z, x, c, y = place()
    me = ((z * n_x + x) * n_c + c) * n_y + y
    return lax.rem(me + step, n_z * n_x * n_c * n_y)


def device_after(step):
    _, n_x, n_c, n_y = sizes()
    index = index_after(step)
    return (
        index // (n_x * n_c * n_y), index // (n_c * n_y) % n_x, index // n_y % n_c, index % n_y
    )


def greet_near():
    n_z = lax.axis_size("z")
    (z, x, c, y), x_near, y_near, c_near = around()
    barrier = pltpu.get_barrier_semaphore()
    for device in (x_near, y_near, c_near):
        pl.semaphore_signal(barrier, inc=1, device_id=device, device_id_type=MESH)

    @pl.when(z > 0)
    def _():
        pl.semaphore_signal(barrier, inc=1, device_id=(z - 1, x, c, y), device_id_type=MESH)

    @pl.when(z < n_z - 1)
    def _():
        pl.semaphore_signal(barrier, inc=1, device_id=(z + 1, x, c, y), device_id_type=MESH)

    pl.semaphore_wait(barrier, 3 + jnp.where(z > 0, 1, 0) + jnp.where(z < n_z - 1, 1, 0))


Z_PIECES = 4


def gather_sems():
    n_z = lax.axis_size("z")
    dma = pltpu.SemaphoreType.DMA
    return [
        dma((n_z, Z_PIECES, 2)), dma((n_z, Z_PIECES)), dma((n_z, 2)), dma((n_z, 2)), dma((n_z, 2)),
        dma((n_z, 2)), dma((n_z, 4)), dma((n_z, 4)), dma,
    ]


def gather_slabs(rows_in, out, sems, work, beside=lambda step: None):
    z_send, z_recv, x_send, x_recv, y_send, y_recv, c_send, c_recv, own_sem = sems
    n_z = lax.axis_size("z")
    half = rows_in.shape[0] // 2
    size = rows_in.shape[0] // Z_PIECES
    (z, x, c, y), x_near, y_near, c_near = around()
    low, high = pl.ds(0, half), pl.ds(half, half)
    everything = pl.ds(0, 2 * half)
    own = pltpu.make_async_copy(rows_in, out.at[z, x, c, y], own_sem)
    own.start()

    def block(origin, px, py, rows):
        return out.at[origin, px, c, py, rows]

    def z_copy(source, origin, index, up):
        rows = pl.ds(index * size, size)
        other = (z + 1, x, c, y) if up else (z - 1, x, c, y)
        return remote(
            source.at[rows], block(origin, x, y, rows), z_send.at[origin, index, 1 if up else 0],
            z_recv.at[origin, index], other,
        )

    def x_copy(source, origin):
        return remote(source, out.at[origin, x, c, y], x_send.at[origin, 0], x_recv.at[origin, 0], x_near)

    def y_copy(source, origin):
        return remote(source, out.at[origin, x, c, y], y_send.at[origin, 0], y_recv.at[origin, 0], y_near)

    def x_relay(origin):
        part = block(origin, x, 1 - y, high)
        return remote(part, part, x_send.at[origin, 1], x_recv.at[origin, 1], x_near)

    def y_relay(origin):
        part = block(origin, 1 - x, y, low)
        return remote(part, part, y_send.at[origin, 1], y_recv.at[origin, 1], y_near)

    def c_copy(source, origin, px, py):
        slot = px * 2 + py
        return remote(
            source, out.at[origin, px, c, py], c_send.at[origin, slot], c_recv.at[origin, slot], c_near
        )

    def column(origin):
        return out.at[origin, x, c, y]

    def spread(source, origin):
        x_copy(source, origin).start()
        y_copy(source, origin).start()
        c_copy(source, origin, x, y).start()

    def relay(origin):
        x_copy(column(origin), origin).wait_recv()
        y_relay(origin).start()
        y_copy(column(origin), origin).wait_recv()
        x_relay(origin).start()
        c_copy(block(origin, 1 - x, y, everything), origin, 1 - x, y).start()
        c_copy(block(origin, x, 1 - y, everything), origin, x, 1 - y).start()

    def finish(origin):
        x_relay(origin).wait_recv()
        y_relay(origin).wait_recv()
        c_copy(block(origin, 1 - x, 1 - y, everything), origin, 1 - x, 1 - y).start()

    def use(origin):
        for px in range(2):
            for py in range(2):
                c_copy(out.at[origin, px, c, py], origin, px, py).wait_recv()
        work(origin)

    def arrive(step):
        below, above = z - step, z + step

        @pl.when(below >= 0)
        def _():
            for index in range(Z_PIECES):
                z_copy(rows_in, below, index, True).wait_recv()

                @pl.when(z < n_z - 1)
                def _():
                    z_copy(column(below), below, index, True).start()

            spread(column(below), below)

        @pl.when(above < n_z)
        def _():
            for index in range(Z_PIECES):
                z_copy(rows_in, above, index, False).wait_recv()

                @pl.when(z > 0)
                def _():
                    z_copy(column(above), above, index, False).start()

            spread(column(above), above)

    for index in range(Z_PIECES):

        @pl.when(z < n_z - 1)
        def _():
            z_copy(rows_in, z, index, True).start()

        @pl.when(z > 0)
        def _():
            z_copy(rows_in, z, index, False).start()

    spread(rows_in, z)
    for step in range(1, n_z + 3):
        if step < n_z:
            arrive(step)
        for action, back in ((relay, 1), (finish, 2), (use, 3)):
            late = step - back
            if late == 0:
                if action is use:
                    own.wait()
                action(z)
            elif 0 < late < n_z:
                for origin in (z - late, z + late):

                    @pl.when((origin >= 0) & (origin < n_z))
                    def _():
                        action(origin)

        beside(step)

    def close(origin, unused):
        x_copy(rows_in, origin).wait_send()
        y_copy(rows_in, origin).wait_send()
        x_relay(origin).wait_send()
        y_relay(origin).wait_send()
        for px in range(2):
            for py in range(2):
                c_copy(out.at[origin, px, c, py], origin, px, py).wait_send()
        for index in range(Z_PIECES):

            @pl.when((z < n_z - 1) & (origin <= z))
            def _():
                z_copy(rows_in, origin, index, True).wait_send()

            @pl.when((z > 0) & (origin >= z))
            def _():
                z_copy(rows_in, origin, index, False).wait_send()

        return unused

    lax.fori_loop(0, n_z, close, 0)


def line_gather_sems():
    n_z = lax.axis_size("z")
    dma = pltpu.SemaphoreType.DMA
    return [dma((n_z, 2, 2)), dma((n_z, 2)), dma((n_z, 2)), dma((n_z, 2)), dma((2,))]


def line_gather(own_parts, all_parts, sems):
    z_send, z_recv, c_send, c_recv, own_sem = sems
    n_z = lax.axis_size("z")
    (z, x, c, y), _, _, c_near = around()
    numbers = range(len(own_parts))

    def z_copy(source, number, origin, up):
        return remote(
            source, all_parts[number](origin, c), z_send.at[origin, number, 1 if up else 0],
            z_recv.at[origin, number], (z + 1, x, c, y) if up else (z - 1, x, c, y),
        )

    def c_copy(source, number, origin):
        return remote(
            source, all_parts[number](origin, c), c_send.at[origin, number], c_recv.at[origin, number], c_near
        )

    own = [
        pltpu.make_async_copy(own_parts[number], all_parts[number](z, c), own_sem.at[number])
        for number in numbers
    ]
    for copy in own:
        copy.start()
    for number in numbers:
        source = own_parts[number]

        @pl.when(z < n_z - 1)
        def _():
            z_copy(source, number, z, True).start()

        @pl.when(z > 0)
        def _():
            z_copy(source, number, z, False).start()

        c_copy(source, number, z).start()

    def beside(step):
        below, above = z - step, z + step

        @pl.when((step >= 1) & (below >= 0))
        def _():
            for number in numbers:
                source = all_parts[number](below, c)
                z_copy(source, number, below, True).wait_recv()

                @pl.when(z < n_z - 1)
                def _():
                    z_copy(source, number, below, True).start()

                c_copy(source, number, below).start()

        @pl.when((step >= 1) & (above < n_z))
        def _():
            for number in numbers:
                source = all_parts[number](above, c)
                z_copy(source, number, above, False).wait_recv()

                @pl.when(z > 0)
                def _():
                    z_copy(source, number, above, False).start()

                c_copy(source, number, above).start()

    def close():
        for copy in own:
            copy.wait()

        def one(origin, unused):
            for number in numbers:
                c_copy(own_parts[number], number, origin).wait()

                @pl.when((z < n_z - 1) & (origin <= z))
                def _():
                    z_copy(own_parts[number], number, origin, True).wait_send()

                @pl.when((z > 0) & (origin >= z))
                def _():
                    z_copy(own_parts[number], number, origin, False).wait_send()

            return unused

        lax.fori_loop(0, n_z, one, 0)

    return beside, close


def line_sems(parts):
    n_z = lax.axis_size("z")
    dma = pltpu.SemaphoreType.DMA
    return [dma((parts,)), dma((parts,)), dma((n_z, 2, parts)), dma((n_z, 2, parts))]


def line_sums(packs, outs, buffers, sems):
    c_send, c_recv, z_send, z_recv = sems
    n_z = lax.axis_size("z")
    (z, x, c, y), _, _, c_near = around()
    numbers = range(len(packs))
    lanes, got, below, above = (buffers[each :: 4] for each in range(4))
    handed = [
        remote(packs[each].at[1 - c], got[each], c_send.at[each], c_recv.at[each], c_near)
        for each in numbers
    ]

    def z_copy(slab, up, each):
        return remote(
            lanes[each].at[slab], (below if up else above)[each].at[slab],
            z_send.at[slab, 1 if up else 0, each], z_recv.at[slab, 1 if up else 0, each],
            (z + 1, x, c, y) if up else (z - 1, x, c, y),
        )

    for copy in handed:
        copy.start()

    def merge():
        for each in numbers:
            handed[each].wait()
            lanes[each][...] = total_of(packs[each][c], got[each][...]).astype(jnp.bfloat16)

    def hop(turn, step):
        high, low = n_z - 1 - turn, turn

        @pl.when((z == step - 1 - turn) & (z < high))
        def _():
            for each in numbers:

                @pl.when(z > 0)
                def _():
                    z_copy(high, True, each).wait_recv()
                    lanes[each][high] = total_of(lanes[each][high], below[each][high]).astype(jnp.bfloat16)

                z_copy(high, True, each).start()

        @pl.when((n_z - 1 - z == step - 1 - turn) & (z > low))
        def _():
            for each in numbers:

                @pl.when(z < n_z - 1)
                def _():
                    z_copy(low, False, each).wait_recv()
                    lanes[each][low] = total_of(lanes[each][low], above[each][low]).astype(jnp.bfloat16)

                z_copy(low, False, each).start()

    def beside(step):
        if step == 1:
            merge()
        if step < n_z:

            def body(turn, unused):
                hop(turn, step)
                return unused

            lax.fori_loop(0, n_z - 1, body, 0)

    def close():
        for each in numbers:
            out = outs[each]
            out[...] = lanes[each][z].astype(jnp.float32)

            @pl.when(z > 0)
            def _():
                z_copy(z, True, each).wait_recv()
                out[...] += below[each][z].astype(jnp.float32)

            @pl.when(z < n_z - 1)
            def _():
                z_copy(z, False, each).wait_recv()
                out[...] += above[each][z].astype(jnp.float32)

        def sent(slab, unused):
            for each in numbers:

                @pl.when(slab > z)
                def _():
                    z_copy(slab, True, each).wait_send()

                @pl.when(slab < z)
                def _():
                    z_copy(slab, False, each).wait_send()

            return unused

        lax.fori_loop(0, n_z, sent, 0)

    return beside, close


def in_pairs(values, slab, px, pc, row):
    return jnp.concatenate([values[slab, px, pc, py, row : row + 1, :] for py in range(2)], axis=1)


def in_lane(values, slab, pc, row):
    return jnp.concatenate([in_pairs(values, slab, px, pc, row) for px in range(2)], axis=1)


def vocab_ids(extent, chunk, shard_rows):
    n_z, n_x, n_c, n_y = sizes()
    z, x, c, y = place()
    me = ((z * n_x + x) * n_c + c) * n_y + y
    rows = lax.broadcasted_iota(jnp.int32, (extent, chunk), 0)
    return rows + me * shard_rows


def logits_kernel(shard_rows, rows_in, table, ints, valid, out, logs, hits, *sems):
    extent = table.shape[0]
    chunk = 2 * rows_in.shape[0]
    scale = table.shape[1] ** (-0.5)
    greet_near()
    hits[...] = jnp.zeros_like(hits)

    def work(slab):
        def one(index, unused):
            px, pc = index // 2, index % 2
            rows = out[slab, px, pc].reshape(chunk, -1)
            value = outer(table[...], rows) * scale
            ids = vocab_ids(extent, chunk, shard_rows)
            inside = lax.broadcasted_iota(jnp.int32, (extent, chunk), 0) < shard_rows
            target = in_pairs(ints, slab, px, pc, 1).astype(jnp.int32)
            shown = in_pairs(valid, slab, px, pc, 0)
            hit = jnp.where(ids == target, value, 0.0)
            hits[...] += jnp.sum(hit, axis=0, keepdims=True) * shown
            value = jnp.where(inside, value, MASKED)
            peak = jnp.max(value, axis=0, keepdims=True)
            log = peak + jnp.log(jnp.sum(jnp.exp(value - peak), axis=0, keepdims=True))
            half = chunk // 2
            logs[slab, px, pc, 0] = log[:, :half]
            logs[slab, px, pc, 1] = log[:, half:]
            return unused

        lax.fori_loop(0, 4, one, 0)

    gather_slabs(rows_in, out, sems, work)


def gather_logits(rows, table, ints, valid, shard_rows, collective_id):
    own, width = rows.shape
    shape = sizes() + (own, width)
    return pl.pallas_call(
        functools.partial(logits_kernel, shard_rows),
        out_shape=(
            jax.ShapeDtypeStruct(shape, rows.dtype),
            jax.ShapeDtypeStruct(sizes() + (1, own), jnp.float32),
            jax.ShapeDtypeStruct((1, 2 * own), jnp.float32),
        ),
        in_specs=[VMEM] * 4,
        out_specs=(VMEM,) * 3,
        scratch_shapes=gather_sems(),
        cost_estimate=pl.CostEstimate(
            flops=0, bytes_accessed=108 * MIB, transcendentals=0
        ),
        compiler_params=pltpu.CompilerParams(
            collective_id=collective_id, has_side_effects=True,
            vmem_limit_bytes=lax.axis_size("z") * 2 * MIB + 20 * MIB,
        ),
    )(rows, table, ints, valid)


def embed_back_kernel(shard_rows, parts, rows_in, ints, table_grad, smalls, *refs):
    packs, refs = refs[:parts], refs[parts:]
    out, small_sum, squares, refs = refs[0], refs[1], refs[2], refs[3:]
    pack_sums, refs = refs[:parts], refs[parts:]
    slabs, small_got, refs = refs[0], refs[1], refs[2:]
    buffers, sems = refs[: 4 * parts], refs[4 * parts :]
    extent = out.shape[0]
    chunk = 2 * rows_in.shape[0]
    small_send, small_recv = sems[-6:-4]
    n_z, n_x, n_c, n_y = sizes()
    count = n_z * n_x * n_c * n_y
    me = index_after(0)
    greet_all()

    def small(step):
        return remote(
            smalls.at[index_after(step)], small_got.at[me], small_send.at[step], small_recv.at[step],
            device_after(step),
        )

    def each(action):
        def body(step, unused):
            action(step)
            return unused

        lax.fori_loop(1, count, body, 0)

    each(lambda step: small(step).start())
    beside, close_line = line_sums(packs, pack_sums, buffers, sems[-4:])
    small_got[me] = smalls[me]
    out[...] = table_grad[...]

    def work(slab):
        for pc in range(2):
            token = in_lane(ints, slab, pc, 0).astype(jnp.int32)
            hot = vocab_ids(extent, 2 * chunk, shard_rows) == token
            hot = jnp.where(hot, 1.0, 0.0).astype(jnp.bfloat16)
            out[...] += matmul(hot, slabs[slab, :, pc].reshape(2 * chunk, -1))

    gather_slabs(rows_in, slabs, sems[:-6], work, beside)
    close_line()
    each(lambda step: small(step).wait())
    small_sum[...] = jnp.sum(small_got[...], axis=0)
    value = out[...]
    inside = lax.broadcasted_iota(jnp.int32, value.shape, 0) < shard_rows
    squares[...] = jnp.sum(jnp.where(inside, value * value, 0.0), axis=0, keepdims=True)
    for part in pack_sums:
        value = part[...].reshape(-1, part.shape[-1])
        squares[:, : part.shape[-1]] += jnp.sum(value * value, axis=0, keepdims=True)


def embed_back(rows, ints, table_grad, smalls, packs, shard_rows, collective_id):
    own, width = rows.shape
    count = smalls.shape[0]
    dma = pltpu.SemaphoreType.DMA
    return pl.pallas_call(
        functools.partial(embed_back_kernel, shard_rows, len(packs)),
        out_shape=(
            jax.ShapeDtypeStruct(table_grad.shape, jnp.float32),
            jax.ShapeDtypeStruct(smalls.shape[1:], jnp.float32),
            jax.ShapeDtypeStruct((1, width), jnp.float32),
        )
        + tuple(jax.ShapeDtypeStruct(pack.shape[2:], jnp.float32) for pack in packs),
        in_specs=[VMEM] * (4 + len(packs)),
        out_specs=(VMEM,) * (3 + len(packs)),
        scratch_shapes=[
            pltpu.VMEM(sizes() + (own, width), rows.dtype), pltpu.VMEM(smalls.shape, jnp.float32),
        ]
        + [pltpu.VMEM(pack.shape[1:], pack.dtype) for pack in packs for _ in range(4)]
        + gather_sems() + [dma((count,)), dma((count,))] + line_sems(len(packs)),
        cost_estimate=pl.CostEstimate(
            flops=0, bytes_accessed=120 * MIB, transcendentals=0
        ),
        compiler_params=pltpu.CompilerParams(
            collective_id=collective_id, has_side_effects=True,
            vmem_limit_bytes=lax.axis_size("z") * 2 * MIB + 28 * MIB,
        ),
    )(rows, ints, table_grad, smalls, *packs)


def slab_order():
    n_z = lax.axis_size("z")
    z = lax.axis_index("z")
    up, down = n_z - 1 - z, z
    longer, shorter = jnp.maximum(up, down), jnp.minimum(up, down)
    far_side = jnp.where(up >= down, 1, -1)

    def target(step):
        late = step - (longer - shorter)
        near_side = jnp.where(late % 2 == 0, far_side, -far_side)
        return jnp.where(
            late < 0, z + far_side * (longer - step), z + near_side * (shorter - late // 2)
        )

    return target


def scatter_scratch(rows, width):
    n_z, n_x, n_c, n_y = sizes()
    half = rows // 2
    low = jnp.bfloat16
    dma = pltpu.SemaphoreType.DMA
    return [
        pltpu.VMEM((n_z, n_x, n_y, rows, width), low),
        pltpu.VMEM((n_z, n_x, n_y, rows, width), low),
        pltpu.VMEM((n_z, n_x, n_y, rows, width), low),
        pltpu.VMEM((n_z, 2, half, width), low),
        pltpu.VMEM((n_z, 2, half, width), low),
        pltpu.VMEM((n_z, half, width), low),
        pltpu.VMEM((n_z, half, width), low),
        pltpu.VMEM((n_z, rows, width), low),
        pltpu.VMEM((n_z, rows, width), low),
        dma((n_z, 2)), dma((n_z, 2)), dma((n_z, 3)), dma((n_z, 3)), dma((n_z, 3)),
        dma((n_z, 3)), dma((n_z, 2)), dma((n_z, 2, 2)),
    ]


def scatter_slabs(out, scratch, before, make, after, beside=lambda step: None):
    (
        lanes, handed, c_got, x_got, y_got, x_last, y_last, below, above,
        c_send, c_recv, x_send, x_recv, y_send, y_recv, z_send, z_recv,
    ) = scratch
    n_z = lax.axis_size("z")
    rows = out.shape[0]
    half = rows // 2
    (z, x, c, y), x_near, y_near, c_near = around()
    halves = (pl.ds(0, half), pl.ds(half, half))
    low, high = halves
    target = slab_order()

    def c_copy(slab, px):
        return remote(
            handed.at[slab, px], c_got.at[slab, px], c_send.at[slab, px], c_recv.at[slab, px], c_near
        )

    def x_first(slab, part):
        block = lanes.at[slab, 1 - x, y if part == 0 else 1 - y, low]
        return remote(block, x_got.at[slab, part], x_send.at[slab, part], x_recv.at[slab, part], x_near)

    def y_first(slab, part):
        block = lanes.at[slab, x if part == 0 else 1 - x, 1 - y, high]
        return remote(block, y_got.at[slab, part], y_send.at[slab, part], y_recv.at[slab, part], y_near)

    def y_second(slab):
        block = lanes.at[slab, x, 1 - y, low]
        return remote(block, y_last.at[slab], y_send.at[slab, 2], y_recv.at[slab, 2], y_near)

    def x_second(slab):
        block = lanes.at[slab, 1 - x, y, high]
        return remote(block, x_last.at[slab], x_send.at[slab, 2], x_recv.at[slab, 2], x_near)

    def z_up(slab, part):
        return remote(
            lanes.at[slab, x, y, halves[part]], below.at[slab, halves[part]], z_send.at[slab, part],
            z_recv.at[slab, 0, part], (z + 1, x, c, y),
        )

    def z_down(slab, part):
        return remote(
            lanes.at[slab, x, y, halves[part]], above.at[slab, halves[part]], z_send.at[slab, part],
            z_recv.at[slab, 1, part], (z - 1, x, c, y),
        )

    def produce(step):
        slab = target(step)
        before(step)

        mine = make(step, slab, 1 - c)
        for px in range(2):
            handed[slab, px] = mine[px]
            c_copy(slab, px).start()
        mine = make(step, slab, c)
        for px in range(2):
            lanes[slab, px] = mine[px]

    def begin(step):
        slab = target(step)
        for px in range(2):
            c_copy(slab, px).wait_recv()

        def merge(px, py):
            lanes[slab, px, py] = total_of(lanes[slab, px, py], c_got[slab, px, py]).astype(jnp.bfloat16)

        merge(1 - x, 1 - y)
        x_first(slab, 1).start()
        y_first(slab, 1).start()
        merge(1 - x, y)
        x_first(slab, 0).start()
        merge(x, 1 - y)
        y_first(slab, 0).start()
        merge(x, y)
        after(step)

    def middle(step):
        slab = target(step)
        x_first(slab, 1).wait_recv()
        x_first(slab, 0).wait_send()
        y_first(slab, 0).wait_send()
        lanes[slab, x, 1 - y, low] = total_of(
            lanes[slab, x, 1 - y, low], x_got[slab, 1]
        ).astype(jnp.bfloat16)
        y_second(slab).start()
        y_first(slab, 1).wait_recv()
        lanes[slab, 1 - x, y, high] = total_of(
            lanes[slab, 1 - x, y, high], y_got[slab, 1]
        ).astype(jnp.bfloat16)
        x_second(slab).start()

    def finish(step):
        slab = target(step)
        for part in range(2):
            if part == 0:
                x_first(slab, 0).wait_recv()
                y_second(slab).wait_recv()
                value = total_of(lanes[slab, x, y, low], x_got[slab, 0], y_last[slab])
            else:
                y_first(slab, 0).wait_recv()
                x_second(slab).wait_recv()
                value = total_of(lanes[slab, x, y, high], y_got[slab, 0], x_last[slab])
            rows_of = halves[part]

            @pl.when(slab > z)
            def _():
                @pl.when(z == 0)
                def _():
                    lanes[slab, x, y, rows_of] = value.astype(jnp.bfloat16)

                @pl.when(z > 0)
                def _():
                    z_up(slab, part).wait_recv()
                    lanes[slab, x, y, rows_of] = total_of(value, below[slab, rows_of]).astype(jnp.bfloat16)

                z_up(slab, part).start()

            @pl.when(slab < z)
            def _():
                @pl.when(z == n_z - 1)
                def _():
                    lanes[slab, x, y, rows_of] = value.astype(jnp.bfloat16)

                @pl.when(z < n_z - 1)
                def _():
                    z_down(slab, part).wait_recv()
                    lanes[slab, x, y, rows_of] = total_of(value, above[slab, rows_of]).astype(jnp.bfloat16)

                z_down(slab, part).start()

            @pl.when(slab == z)
            def _():
                out[rows_of, :] = value

                @pl.when(z > 0)
                def _():
                    z_up(slab, part).wait_recv()
                    out[rows_of, :] += below[slab, rows_of].astype(jnp.float32)

                @pl.when(z < n_z - 1)
                def _():
                    z_down(slab, part).wait_recv()
                    out[rows_of, :] += above[slab, rows_of].astype(jnp.float32)

    def turn(step, unused):
        for action, back in ((produce, 0), (begin, 0), (middle, 1), (finish, 2)):

            @pl.when((step >= back) & (step < n_z + back))
            def _():
                action(step - back)

        beside(step)
        return unused

    lax.fori_loop(0, n_z + 2, turn, 0)

    def close(slab, unused):
        for px in range(2):
            c_copy(slab, px).wait_send()
        x_first(slab, 1).wait_send()
        y_first(slab, 1).wait_send()
        x_second(slab).wait_send()
        y_second(slab).wait_send()
        for part in range(2):

            @pl.when(slab > z)
            def _():
                z_up(slab, part).wait_send()

            @pl.when(slab < z)
            def _():
                z_down(slab, part).wait_send()

        return unused

    lax.fori_loop(0, n_z, close, 0)


def embed_kernel(shard_rows, table, ints, qkv_own, out_own, out, qkv_all, out_all, *scratch):
    extent = table.shape[0]
    chunk = 2 * out.shape[0]
    greet_near()
    beside, close = line_gather(
        (qkv_own, out_own),
        (lambda pz, pc: qkv_all.at[:, pz, :, pc], lambda pz, pc: out_all.at[:, pz, pc]),
        scratch[-5:],
    )

    def make(step, slab, pc):
        token = in_lane(ints, slab, pc, 0).astype(jnp.int32)
        hot = vocab_ids(extent, 2 * chunk, shard_rows) == token
        hot = jnp.where(hot, 1.0, 0.0).astype(jnp.bfloat16)
        return inner(hot, table[...]).astype(jnp.bfloat16).reshape(2, 2, chunk // 2, -1)

    scatter_slabs(out, scratch[:-5], lambda step: None, make, lambda step: None, beside)
    close()


def embed(table, ints, qkv_own, out_own, own, shard_rows, collective_id):
    width = table.shape[1]
    n_z, n_x, n_c, _ = sizes()
    layers = qkv_own.shape[0]
    return pl.pallas_call(
        functools.partial(embed_kernel, shard_rows),
        out_shape=(
            jax.ShapeDtypeStruct((own, width), jnp.float32),
            jax.ShapeDtypeStruct((layers, n_z, n_x, n_c) + qkv_own.shape[2:], qkv_own.dtype),
            jax.ShapeDtypeStruct((layers, n_z, n_c) + out_own.shape[1:], out_own.dtype),
        ),
        in_specs=[VMEM] * 4,
        out_specs=(VMEM,) * 3,
        scratch_shapes=scatter_scratch(own, width) + line_gather_sems(),
        cost_estimate=pl.CostEstimate(
            flops=0, bytes_accessed=120 * MIB, transcendentals=0
        ),
        compiler_params=pltpu.CompilerParams(
            collective_id=collective_id, has_side_effects=True,
            vmem_limit_bytes=lax.axis_size("z") * 3 * MIB + 12 * MIB,
        ),
    )(table, ints, qkv_own, out_own)


def vocab_back_kernel(
    shard_rows, held, rows_all, table, ints, logs, weights, out, table_grad, slab_rows, changes, slab_sem, *scratch
):
    extent, width = table.shape
    chunk = 2 * out.shape[0]
    scale = width ** (-0.5)
    n_z = lax.axis_size("z")
    target = slab_order()

    def load(step):
        return pltpu.make_async_copy(
            rows_all.at[target(step)], slab_rows.at[step % 2], slab_sem.at[step % 2]
        )

    if not held:
        load(0).start()
    greet_near()
    table_grad[...] = jnp.zeros_like(table_grad)

    def rows_of(step, pc):
        if held:
            return rows_all[target(step), :, pc].reshape(2 * chunk, width)
        return slab_rows[step % 2, :, pc].reshape(2 * chunk, width)

    def before(step):
        if held:
            return
        load(step).wait()

        @pl.when(step + 1 < n_z)
        def _():
            load(step + 1).start()

    def make(step, slab, pc):
        value = outer(table[...], rows_of(step, pc)) * scale
        aim = in_lane(ints, slab, pc, 1).astype(jnp.int32)
        hot = jnp.where(vocab_ids(extent, 2 * chunk, shard_rows) == aim, 1.0, 0.0)
        change = jnp.exp(value - in_lane(logs, slab, pc, 0)) - hot
        change = (change * in_lane(weights, slab, pc, 0)).astype(jnp.bfloat16)
        changes[pc] = change
        return (inner(change, table[...]) * scale).astype(jnp.bfloat16).reshape(2, 2, chunk // 2, width)

    def after(step):
        for pc in range(2):
            table_grad[...] += matmul(changes[pc], rows_of(step, pc))

    scatter_slabs(out, scratch, before, make, after)
    table_grad[...] = table_grad[...] * scale


def vocab_back(rows_all, table, ints, logs, weights, shard_rows, collective_id):
    own, width = rows_all.shape[4:]
    extent = table.shape[0]
    n_z, n_x, n_c, n_y = sizes()
    held = n_z <= 4
    return pl.pallas_call(
        functools.partial(vocab_back_kernel, shard_rows, held),
        out_shape=(
            jax.ShapeDtypeStruct((own, width), jnp.float32),
            jax.ShapeDtypeStruct((extent, width), jnp.float32),
        ),
        in_specs=[VMEM if held else ANY] + [VMEM] * 4,
        out_specs=(VMEM,) * 2,
        scratch_shapes=[
            pltpu.VMEM((1,) * 6 if held else (2, n_x, n_c, n_y, own, width), rows_all.dtype),
            pltpu.VMEM((n_c, extent, 4 * own), jnp.bfloat16),
            pltpu.SemaphoreType.DMA((2,)),
        ] + scatter_scratch(own, width),
        cost_estimate=pl.CostEstimate(
            flops=0, bytes_accessed=144 * MIB, transcendentals=0
        ),
        compiler_params=pltpu.CompilerParams(
            collective_id=collective_id, has_side_effects=True,
            vmem_limit_bytes=n_z * 3 * MIB + 24 * MIB if n_z <= 8 else 62 * MIB,
        ),
    )(rows_all, table, ints, logs, weights)


SQRT_HALF = 0.5**0.5
DENSITY = 0.3989422804014327


def matmul(left, right):
    return jnp.dot(left, right, preferred_element_type=jnp.float32)


def inner(left, right):
    return lax.dot_general(
        left, right, (((0,), (0,)), ((), ())), preferred_element_type=jnp.float32
    )


def outer(left, right):
    return lax.dot_general(
        left, right, (((1,), (1,)), ((), ())), preferred_element_type=jnp.float32
    )


def plane_gather(own_rows, blocks, send_sem, recv_sem):
    half = own_rows.shape[0] // 2
    (z, x, c, y), x_near, y_near, _ = around()
    low, high = pl.ds(0, half), pl.ds(half, half)

    def copy(slot, px, py, rows, source, device):
        target = blocks.at[px, py, rows]
        return remote(target if source is None else source.at[rows], target, send_sem.at[slot], recv_sem.at[slot], device)

    first = [
        copy(0, x, y, low, own_rows, x_near),
        copy(1, x, y, high, own_rows, y_near),
        copy(2, x, y, high, own_rows, x_near),
        copy(3, x, y, low, own_rows, y_near),
    ]
    relays = [copy(4, 1 - x, y, low, None, y_near), copy(5, x, 1 - y, high, None, x_near)]
    for each in first:
        each.start()

    def wait_near():
        first[0].wait_recv()
        relays[0].start()
        first[1].wait_recv()
        relays[1].start()

    def wait_x():
        first[2].wait_recv()

    def wait_y():
        first[3].wait_recv()

    def wait_diagonal():
        for each in relays:
            each.wait_recv()

    def close():
        for each in first + relays:
            each.wait_send()

    return wait_near, wait_x, wait_y, wait_diagonal, close


def plane_sum(parts, got, out, send_sem, recv_sem):
    (z, x, c, y), x_near, y_near, _ = around()
    diagonal = (z, 1 - x, c, 1 - y)
    copies = [
        remote(parts.at[device[1], device[3]], got.at[slot], send_sem.at[slot], recv_sem.at[slot], device)
        for slot, device in enumerate((x_near, y_near, diagonal))
    ]

    def close():
        for each in copies:
            each.wait_recv()
        out[...] = total_of(parts[x, y], got[0], got[1], got[2])
        for each in copies:
            each.wait_send()

    return copies, close


def order_experts(kept, got, ordered, sems):
    n_z, n_c, _, depth, _ = kept.shape
    x = lax.axis_index("x")
    copies = []
    for pz in range(n_z):
        for pc in range(n_c):
            for side, weights in enumerate((kept, got)):
                if depth == ordered.shape[1]:
                    rows, side = pl.ds(0, depth), 0
                else:
                    px = x if side == 0 else 1 - x
                    at = (pz * 2 + px) * n_c + pc
                    rows = pl.ds(pl.multiple_of(at * depth, 16), depth)
                slot = (pz * n_c + pc) * 2 + side
                if depth == ordered.shape[1] and weights is got:
                    continue
                copies.append(
                    pltpu.make_async_copy(weights.at[pz, pc], ordered.at[:, rows], sems.at[slot])
                )
    for copy in copies:
        copy.start()
    return copies


def experts_kernel(
    own_rows, route, w_kept, w_got, out, wide, before, hidden, ordered, parts, got, w_sem, g_send, g_recv, s_send, s_recv
):
    (z, x, c, y), x_near, y_near, _ = around()
    diagonal = (z, 1 - x, c, 1 - y)
    loads = order_experts(w_kept, w_got, ordered, w_sem)
    up, down = ordered.at[pl.ds(0, 2)], ordered.at[pl.ds(2, 2)]
    greet((x_near, y_near, diagonal))
    wait_near, wait_x, wait_y, wait_diagonal, close = plane_gather(own_rows, wide, g_send, g_recv)
    copies, finish = plane_sum(parts, got, out, s_send, s_recv)
    wide[x, y] = own_rows[...]

    def work(px, py):
        rows = wide[px, py]
        first = route[px, py] == 0
        value = jnp.where(first, matmul(rows, up[0]), matmul(rows, up[1]))
        before[px, py] = value
        active = 0.5 * value * (1.0 + lax.erf(value * SQRT_HALF))
        hidden_first = jnp.where(first, active, 0.0).astype(jnp.bfloat16)
        hidden_second = jnp.where(first, 0.0, active).astype(jnp.bfloat16)
        hidden[px, py] = active.astype(jnp.bfloat16)
        total = outer(hidden_first, down[0]) + outer(hidden_second, down[1])
        parts[px, py] = total.astype(jnp.bfloat16)

    for load in loads:
        load.wait()
    work(x, y)
    wait_near()
    wait_x()
    work(1 - x, y)
    copies[0].start()
    wait_y()
    work(x, 1 - y)
    copies[1].start()
    wait_diagonal()
    work(1 - x, 1 - y)
    copies[2].start()
    finish()
    close()


def experts(own_rows, route, weights, collective_id):
    _, n_x, _, n_y = sizes()
    own, width = own_rows.shape
    wide = weights[0].shape[4]
    dma = pltpu.SemaphoreType.DMA
    low = jnp.bfloat16
    return pl.pallas_call(
        experts_kernel,
        out_shape=(
            jax.ShapeDtypeStruct((own, width), jnp.float32),
            jax.ShapeDtypeStruct((n_x, n_y, own, width), low),
            jax.ShapeDtypeStruct((n_x, n_y, own, wide), jnp.float32),
            jax.ShapeDtypeStruct((n_x, n_y, own, wide), low),
        ),
        in_specs=[VMEM, VMEM, HBM, HBM],
        out_specs=(VMEM,) * 4,
        scratch_shapes=[
            pltpu.VMEM((4, width, wide), low),
            pltpu.VMEM((n_x, n_y, own, width), low),
            pltpu.VMEM((3, own, width), low),
            dma((width // weights[0].shape[3],)), dma((6,)), dma((6,)), dma((3,)), dma((3,)),
        ],
        compiler_params=pltpu.CompilerParams(
            collective_id=collective_id, has_side_effects=True, vmem_limit_bytes=20 * MIB
        ),
        cost_estimate=pl.CostEstimate(
            flops=8 * own * 4 * width * wide, bytes_accessed=54 * MIB, transcendentals=4 * own * wide
        ),
    )(own_rows, route, *weights)


def experts_back_kernel(
    own_rows, route, w_kept, w_got, wide_kept, before_kept, hidden_kept, out, grads,
    ordered, wide, before, hidden, made, wide_grad, before_grad, parts, got,
    w_sem, k_sem, o_sem, g_send, g_recv, s_send, s_recv,
):
    (z, x, c, y), x_near, y_near, _ = around()
    diagonal = (z, 1 - x, c, 1 - y)
    loads = order_experts(w_kept, w_got, ordered, w_sem)
    for slot, (source, target) in enumerate(
        ((before_kept, before), (wide_kept, wide), (hidden_kept, hidden))
    ):
        load = pltpu.make_async_copy(source, target, k_sem.at[slot])
        load.start()
        loads.append(load)
    up, down = ordered.at[pl.ds(0, 2)], ordered.at[pl.ds(2, 2)]
    greet((x_near, y_near, diagonal))
    wait_near, wait_x, wait_y, wait_diagonal, close = plane_gather(own_rows, wide_grad, g_send, g_recv)
    copies, finish = plane_sum(parts, got, out, s_send, s_recv)
    wide_grad[x, y] = own_rows[...]

    def work(px, py):
        rows = wide_grad[px, py]
        first = route[px, py] == 0
        hidden_grad = jnp.where(first, matmul(rows, down[0]), matmul(rows, down[1]))
        value = before[px, py]
        slope = 0.5 * (1.0 + lax.erf(value * SQRT_HALF)) + value * (
            DENSITY * jnp.exp(-0.5 * value * value)
        )
        change = (hidden_grad * slope).astype(jnp.bfloat16)
        before_grad[px, py] = change
        change_first = jnp.where(first, change, 0)
        change_second = jnp.where(first, 0, change)
        total = outer(change_first, up[0]) + outer(change_second, up[1])
        parts[px, py] = total.astype(jnp.bfloat16)

    for load in loads:
        load.wait()
    work(x, y)
    wait_near()
    wait_x()
    work(1 - x, y)
    copies[0].start()
    wait_y()
    work(x, 1 - y)
    copies[1].start()
    wait_diagonal()
    work(1 - x, 1 - y)
    copies[2].start()
    close()

    lane = 4 * own_rows.shape[0]
    rows = wide[...].reshape(lane, -1)
    grad_rows = wide_grad[...].reshape(lane, -1)
    first = route[...].reshape(lane, 1) == 0
    change = before_grad[...].reshape(lane, -1)
    active = hidden[...].reshape(lane, -1)
    low = jnp.bfloat16
    n_z, n_x, n_c, _ = sizes()
    depth = grads.shape[3]
    saves = []

    def keep(slot, value):
        value = value.astype(low)
        for pz in range(n_z):
            for px in range(n_x):
                for pc in range(n_c):
                    start = ((pz * n_x + px) * n_c + pc) * depth
                    made[slot, pz * n_c + pc, px] = value[start : start + depth]
        save = pltpu.make_async_copy(made.at[slot], grads.at[:, :, slot], o_sem.at[slot])
        save.start()
        saves.append(save)

    keep(0, inner(rows, jnp.where(first, change, 0)))
    keep(1, inner(rows, jnp.where(first, 0, change)))
    keep(2, inner(grad_rows, jnp.where(first, active, 0)))
    keep(3, inner(grad_rows, jnp.where(first, 0, active)))
    finish()
    for save in saves:
        save.wait()


def experts_back(own_rows, route, weights, wide, before, hidden, collective_id):
    n_z, n_x, n_c, n_y = sizes()
    own, width = own_rows.shape
    units = weights[0].shape[4]
    dma = pltpu.SemaphoreType.DMA
    low = jnp.bfloat16
    return pl.pallas_call(
        experts_back_kernel,
        out_shape=(
            jax.ShapeDtypeStruct((own, width), jnp.float32),
            jax.ShapeDtypeStruct((n_z * n_c, n_x, 4, width // (n_z * n_x * n_c), units), low),
        ),
        in_specs=[VMEM, VMEM] + [HBM] * 5,
        out_specs=(VMEM, HBM),
        scratch_shapes=[
            pltpu.VMEM((4, width, units), low),
            pltpu.VMEM(wide.shape, wide.dtype), pltpu.VMEM(before.shape, before.dtype),
            pltpu.VMEM(hidden.shape, hidden.dtype),
            pltpu.VMEM((4, n_z * n_c, n_x, width // (n_z * n_x * n_c), units), low),
            pltpu.VMEM((n_x, n_y, own, width), low),
            pltpu.VMEM((n_x, n_y, own, units), low),
            pltpu.VMEM((n_x, n_y, own, width), low),
            pltpu.VMEM((3, own, width), low),
            dma((width // weights[0].shape[3],)), dma((3,)), dma((4,)), dma((6,)), dma((6,)), dma((3,)), dma((3,)),
        ],
        compiler_params=pltpu.CompilerParams(
            collective_id=collective_id, has_side_effects=True, vmem_limit_bytes=34 * MIB
        ),
        cost_estimate=pl.CostEstimate(
            flops=16 * own * 4 * width * units, bytes_accessed=54 * MIB, transcendentals=8 * own * units
        ),
    )(own_rows, route, *weights, wide, before, hidden)


def in_owner_order(value, target):
    value = value.astype(target.dtype)
    n_c, n_z = target.shape[:2]
    n_x = target.shape[2] if len(target.shape) == 5 else 1
    depth = target.shape[-2]
    for pz in range(n_z):
        for px in range(n_x):
            for pc in range(n_c):
                start = ((pz * n_x + px) * n_c + pc) * depth
                if len(target.shape) == 5:
                    target[pc, pz, px] = value[start : start + depth]
                else:
                    target[pc, pz] = value[start : start + depth]


def project_kernel(transposed, with_grad, *refs):
    if with_grad:
        rows, weight, left, out, grad, parts, got, s_send, s_recv = refs
    else:
        rows, weight, out, parts, got, s_send, s_recv = refs
    (z, x, c, y), x_near, y_near, _ = around()
    diagonal = (z, 1 - x, c, 1 - y)
    barrier = pltpu.get_barrier_semaphore()
    for device in (x_near, y_near, diagonal):
        pl.semaphore_signal(barrier, inc=1, device_id=device, device_id_type=MESH)
    copies, finish = plane_sum(parts, got, out, s_send, s_recv)

    def work(px, py):
        times = outer if transposed else matmul
        parts[px, py] = times(rows[px, py], weight[...]).astype(jnp.bfloat16)

    work(1 - x, 1 - y)
    pl.semaphore_wait(barrier, 3)
    copies[2].start()
    work(1 - x, y)
    copies[0].start()
    work(x, 1 - y)
    copies[1].start()
    work(x, y)
    if with_grad:
        lane = 4 * out.shape[0]
        in_owner_order(inner(left[...].reshape(lane, -1), rows[...].reshape(lane, -1)), grad)
    finish()


def project(rows, weight, transposed, left, collective_id):
    n_x, n_y, own, depth = rows.shape
    n_z, _, n_c, _ = sizes()
    width = weight.shape[0] if transposed else weight.shape[1]
    low = jnp.bfloat16
    dma = pltpu.SemaphoreType.DMA
    return pl.pallas_call(
        functools.partial(project_kernel, transposed, left is not None),
        out_shape=(jax.ShapeDtypeStruct((own, width), jnp.float32),)
        + (
            ()
            if left is None
            else (
                jax.ShapeDtypeStruct(
                    (n_c, n_z, n_x, left.shape[3] // (n_z * n_x * n_c), depth), low
                ),
            )
        ),
        in_specs=[VMEM] * (2 if left is None else 3),
        out_specs=(VMEM,) * (1 if left is None else 2),
        scratch_shapes=[
            pltpu.VMEM((n_x, n_y, own, width), low), pltpu.VMEM((3, own, width), low), dma((3,)), dma((3,)),
        ],
        compiler_params=pltpu.CompilerParams(
            collective_id=collective_id, has_side_effects=True, vmem_limit_bytes=16 * MIB
        ),
        cost_estimate=pl.CostEstimate(
            flops=8 * own * width * depth, bytes_accessed=24 * MIB, transcendentals=0
        ),
    )(rows, weight, *(() if left is None else (left,)))


def gather_project_kernel(transposed, split, with_grad, own_rows, weight, *rest):
    if with_grad:
        left, wide, rest = rest[0], rest[1], (rest[0],) + rest[2:]
    else:
        wide, rest = rest[0], rest[1:]

    (z, x, c, y), x_near, y_near, _ = around()
    rest, (g_send, g_recv) = rest[:-2], rest[-2:]
    left, outs = (rest[0], rest[1:]) if with_grad else (None, rest)
    greet((x_near, y_near))
    wait_near, wait_x, wait_y, wait_diagonal, close = plane_gather(own_rows, wide, g_send, g_recv)
    wide[x, y] = own_rows[...]

    def work(px, py):
        times = outer if transposed else matmul
        value = times(wide[px, py], weight[...]).astype(jnp.bfloat16)
        start = 0
        for out, size in zip(outs, split):
            out[px, py] = value[:, start : start + size]
            start += size

    work(x, y)
    wait_near()
    wait_x()
    work(1 - x, y)
    wait_y()
    work(x, 1 - y)
    wait_diagonal()
    work(1 - x, 1 - y)
    if with_grad:
        lane = 4 * own_rows.shape[0]
        in_owner_order(inner(left[...], wide[...].reshape(lane, -1)), outs[-1])
    close()


def gather_project(own_rows, weight, transposed, split, left, collective_id):
    n_z, n_x, n_c, n_y = sizes()
    own, width = own_rows.shape
    depth = weight.shape[0] if transposed else weight.shape[1]
    dma = pltpu.SemaphoreType.DMA
    low = jnp.bfloat16
    return pl.pallas_call(
        functools.partial(gather_project_kernel, transposed, split, left is not None),
        out_shape=(
            jax.ShapeDtypeStruct((n_x, n_y, own, width), low),
        ) + tuple(jax.ShapeDtypeStruct((n_x, n_y, own, size), low) for size in split)
        + (
            ()
            if left is None
            else (jax.ShapeDtypeStruct((n_c, n_z, left.shape[1] // (n_z * n_c), width), low),)
        ),
        in_specs=[VMEM] * (2 if left is None else 3),
        out_specs=(VMEM,) * (1 + len(split) + (0 if left is None else 1)),
        scratch_shapes=[dma((6,)), dma((6,))],
        compiler_params=pltpu.CompilerParams(
            collective_id=collective_id, has_side_effects=True, vmem_limit_bytes=12 * MIB
        ),
        cost_estimate=pl.CostEstimate(
            flops=8 * own * width * depth, bytes_accessed=24 * MIB, transcendentals=0
        ),
    )(own_rows, weight, *(() if left is None else (left,)))


def merge_logs_kernel(source, out, got, mine, send_one, recv_one, send_two, recv_two):
    n_z, n_x, n_c, n_y = sizes()
    count = n_z * n_x * n_c * n_y
    z, x, c, y = place()
    me = ((z * n_x + x) * n_c + c) * n_y + y

    def device_of(index):
        return (
            index // (n_x * n_c * n_y), index // (n_c * n_y) % n_x, index // n_y % n_c, index % n_y
        )

    barrier = pltpu.get_barrier_semaphore()

    def call(step, unused):
        other = lax.rem(me + step, count)
        pl.semaphore_signal(barrier, inc=1, device_id=device_of(other), device_id_type=MESH)
        return unused

    lax.fori_loop(1, count, call, 0)
    got[me] = source[me]
    pl.semaphore_wait(barrier, count - 1)

    def first(step):
        other = lax.rem(me + step, count)
        return remote(
            source.at[other], got.at[me], send_one.at[step], recv_one.at[step], device_of(other)
        )

    def second(step):
        other = lax.rem(me + step, count)
        return remote(mine, out.at[me], send_two.at[step], recv_two.at[step], device_of(other))

    def each(action):
        def body(step, unused):
            action(step)
            return unused

        lax.fori_loop(1, count, body, 0)

    each(lambda step: first(step).start())
    each(lambda step: first(step).wait())
    values = got[...]
    peak = jnp.max(values, axis=0)
    mine[...] = peak + jnp.log(jnp.sum(jnp.exp(values - peak[None]), axis=0))
    out[me] = mine[...]
    each(lambda step: second(step).start())
    each(lambda step: second(step).wait())


def merge_logs(blocks, collective_id):
    count = blocks.shape[0]
    dma = pltpu.SemaphoreType.DMA
    return pl.pallas_call(
        merge_logs_kernel,
        out_shape=jax.ShapeDtypeStruct(blocks.shape, blocks.dtype),
        in_specs=[VMEM],
        out_specs=VMEM,
        scratch_shapes=[
            pltpu.VMEM(blocks.shape, blocks.dtype), pltpu.VMEM(blocks.shape[1:], blocks.dtype),
            dma((count,)), dma((count,)), dma((count,)), dma((count,)),
        ],
        cost_estimate=pl.CostEstimate(
            flops=0, bytes_accessed=42 * MIB, transcendentals=0
        ),
        compiler_params=pltpu.CompilerParams(
            collective_id=collective_id, has_side_effects=True, vmem_limit_bytes=8 * MIB
        ),
    )(blocks)


def key_position(index, part, chunk):
    lane = 2 * chunk
    start = (part // 2) * (2 * lane) + (part % 2) * chunk
    return start + index + jnp.where(index >= chunk, chunk, 0)


def as_column(row):
    wide_row = jnp.broadcast_to(row.astype(jnp.float32), (8, row.shape[1]))
    return wide_row.T[:, :1].astype(jnp.int32)


def near_shown(side, chunk, query_pos, query_seg, near_pos, near_seg):
    columns = slice(side * chunk, (side + 1) * chunk)
    rows = slice(2 * side * chunk, 2 * (side + 1) * chunk)
    shown = (
        (near_seg[rows, :] == query_seg[:, columns])
        & (near_pos[rows, :] <= query_pos[:, columns])
        & (near_pos[rows, :] >= PROMPT)
    )
    return columns, rows, shown


def attend_kernel(
    chunk, query, far, near, query_pos, query_seg, near_pos, near_seg,
    out, out_low, log_total, scores, far_t, near_t,
):
    lane, feature = query.shape
    group = feature // HEAD_DIM
    prompt_rows = far.shape[0]
    parts = prompt_rows // lane
    query_t = (query[...].astype(jnp.float32) * HEAD_DIM ** (-0.5)).T.astype(jnp.bfloat16)
    far_t[...] = far[...].astype(jnp.float32).T.astype(jnp.bfloat16)
    near_t[...] = near[...].astype(jnp.float32).T.astype(jnp.bfloat16)
    row_of = lax.broadcasted_iota(jnp.int32, (feature, lane), 0)
    q_pos = query_pos[...]
    near_pos, near_seg = as_column(near_pos[...]), as_column(near_seg[...])

    for head in range(group):
        low, high = head * HEAD_DIM, (head + 1) * HEAD_DIM
        query_h = jnp.where((row_of >= low) & (row_of < high), query_t, 0)

        def score_part(part, peak):
            block = far[pl.ds(pl.multiple_of(part * lane, lane), lane), :feature]
            value = matmul(block, query_h)
            index = lax.broadcasted_iota(jnp.int32, (lane, lane), 0)
            value = jnp.where(key_position(index, part, chunk) <= q_pos, value, MASKED)
            scores[pl.ds(pl.multiple_of(part * lane, lane), lane), :] = value
            return jnp.maximum(peak, jnp.max(value, axis=0, keepdims=True))

        peak = lax.fori_loop(0, parts, score_part, jnp.full((1, lane), MASKED, jnp.float32))
        near_peaks = []
        for side in range(2):
            columns, rows, shown = near_shown(side, chunk, query_pos, query_seg, near_pos, near_seg)
            value = matmul(near[rows, :feature], query_h[:, columns])
            value = jnp.where(shown, value, MASKED)
            scores[prompt_rows : prompt_rows + lane, columns] = value
            near_peaks.append(jnp.max(value, axis=0, keepdims=True))
        peak = jnp.maximum(peak, jnp.concatenate(near_peaks, axis=1))

        def weigh_part(part, state):
            total, mixed = state
            start = pl.multiple_of(part * lane, lane)
            chance = jnp.exp(scores[pl.ds(start, lane), :] - peak)
            total = total + jnp.sum(chance, axis=0, keepdims=True)
            mixed = mixed + matmul(
                far_t[feature + low : feature + high, pl.ds(start, lane)],
                chance.astype(jnp.bfloat16),
            )
            return total, mixed

        total, mixed = lax.fori_loop(
            0,
            parts,
            weigh_part,
            (jnp.zeros((1, lane), jnp.float32), jnp.zeros((HEAD_DIM, lane), jnp.float32)),
        )
        near_total, near_mixed = [], []
        for side in range(2):
            columns = slice(side * chunk, (side + 1) * chunk)
            rows = slice(side * lane, (side + 1) * lane)
            chance = jnp.exp(scores[prompt_rows : prompt_rows + lane, columns] - peak[:, columns])
            near_total.append(jnp.sum(chance, axis=0, keepdims=True))
            near_mixed.append(
                matmul(near_t[feature + low : feature + high, rows], chance.astype(jnp.bfloat16))
            )
        total = total + jnp.concatenate(near_total, axis=1)
        mixed = mixed + jnp.concatenate(near_mixed, axis=1)
        out[low:high, :] = mixed / total
        log_total[head : head + 1, :] = peak + jnp.log(total)
    out_low[...] = out[...].T.astype(jnp.bfloat16)


def attend(queries, far, near, places, chunk):
    lane, feature = queries.shape
    prompt_rows = far.shape[0]
    group = feature // HEAD_DIM
    total_rows = prompt_rows + lane
    return pl.pallas_call(
        functools.partial(attend_kernel, chunk),
        out_shape=(
            jax.ShapeDtypeStruct((feature, lane), jnp.float32),
            jax.ShapeDtypeStruct((lane, feature), jnp.bfloat16),
            jax.ShapeDtypeStruct((group, lane), jnp.float32),
        ),
        in_specs=[VMEM] * 7,
        out_specs=(VMEM,) * 3,
        scratch_shapes=[
            pltpu.VMEM((total_rows, lane), jnp.float32),
            pltpu.VMEM((2 * feature, prompt_rows), jnp.bfloat16),
            pltpu.VMEM((2 * feature, 2 * lane), jnp.bfloat16),
        ],
        compiler_params=pltpu.CompilerParams(vmem_limit_bytes=20 * MIB),
        cost_estimate=pl.CostEstimate(
            flops=8 * group * lane * total_rows * 128,
            bytes_accessed=8 * MIB,
            transcendentals=group * lane * total_rows,
        ),
    )(queries, far, near, *places)


def attend_back_kernel(
    chunk, query, far, near, query_pos, query_seg, near_pos, near_seg,
    log_total, mixed, answer, query_grad, far_grad, near_grad,
    far_t, near_t, far_values, near_values, far_sum, near_sum, query_sum,
):
    lane, feature = query.shape
    group = feature // HEAD_DIM
    prompt_rows = far.shape[0]
    parts = prompt_rows // lane
    scaled = (query[...].astype(jnp.float32) * HEAD_DIM ** (-0.5)).astype(jnp.bfloat16)
    query_t = scaled.astype(jnp.float32).T.astype(jnp.bfloat16)
    answers = answer[...]
    answer_t = answers.astype(jnp.float32).T.astype(jnp.bfloat16)
    far_t[...] = far[:, :feature].astype(jnp.float32).T.astype(jnp.bfloat16)
    near_t[...] = near[:, :feature].astype(jnp.float32).T.astype(jnp.bfloat16)
    far_values[...] = far[:, feature:]
    near_values[...] = near[:, feature:]
    row_of = lax.broadcasted_iota(jnp.int32, (feature, lane), 0)
    column_of = lax.broadcasted_iota(jnp.int32, (lane, feature), 1)
    q_pos = query_pos[...]
    near_pos, near_seg = as_column(near_pos[...]), as_column(near_seg[...])

    for head in range(group):
        low, high = head * HEAD_DIM, (head + 1) * HEAD_DIM
        in_rows = (row_of >= low) & (row_of < high)
        in_columns = (column_of >= low) & (column_of < high)
        query_ht = jnp.where(in_rows, query_t, 0)
        answer_ht = jnp.where(in_rows, answer_t, 0)
        query_h = jnp.where(in_columns, scaled, 0)
        answer_h = jnp.where(in_columns, answers, 0)
        log_h = log_total[head : head + 1, :]
        delta_h = jnp.sum(
            answer_t[low:high, :].astype(jnp.float32) * mixed[low:high, :], axis=0, keepdims=True
        )

        def slopes(key_block, value_block, shown, columns):
            value = matmul(key_block, query_ht[:, columns])
            chance = jnp.exp(jnp.where(shown, value - log_h[:, columns], MASKED))
            slope = matmul(value_block, answer_ht[:, columns])
            change = (chance * (slope - delta_h[:, columns])).astype(jnp.bfloat16)
            chance = chance.astype(jnp.bfloat16)
            return change, matmul(change, query_h[columns]), matmul(chance, answer_h[columns])

        def add(sums, rows, key_part, value_part):
            if head == 0:
                sums[0, rows, :] = key_part
                sums[1, rows, :] = value_part
            else:
                sums[0, rows, :] += key_part
                sums[1, rows, :] += value_part

        def back_part(part, total):
            rows = pl.ds(pl.multiple_of(part * lane, lane), lane)
            index = lax.broadcasted_iota(jnp.int32, (lane, lane), 0)
            shown = key_position(index, part, chunk) <= q_pos
            change, key_part, value_part = slopes(
                far[rows, :feature], far_values[rows, :], shown, slice(0, lane)
            )
            add(far_sum, rows, key_part, value_part)
            return total + matmul(far_t[low:high, rows], change)

        total = lax.fori_loop(0, parts, back_part, jnp.zeros((HEAD_DIM, lane), jnp.float32))
        near_total = []
        for side in range(2):
            columns, rows, shown = near_shown(side, chunk, query_pos, query_seg, near_pos, near_seg)
            change, key_part, value_part = slopes(
                near[rows, :feature], near_values[rows, :], shown, columns
            )
            add(near_sum, rows, key_part, value_part)
            near_total.append(matmul(near_t[low:high, rows], change))
        query_sum[low:high, :] = (total + jnp.concatenate(near_total, axis=1)) * HEAD_DIM ** (-0.5)
    query_grad[...] = query_sum[...].T.astype(jnp.bfloat16)
    for sums, grad in ((far_sum, far_grad), (near_sum, near_grad)):
        grad[...] = jnp.concatenate(
            [sums[0].astype(jnp.bfloat16), sums[1].astype(jnp.bfloat16)], axis=1
        )


def attend_back(queries, far, near, places, log_total, mixed, answer, chunk):
    lane, feature = queries.shape
    prompt_rows = far.shape[0]
    group = feature // HEAD_DIM
    total_rows = prompt_rows + lane
    low = jnp.bfloat16
    return pl.pallas_call(
        functools.partial(attend_back_kernel, chunk),
        out_shape=(
            jax.ShapeDtypeStruct((lane, feature), low),
            jax.ShapeDtypeStruct((prompt_rows, 2 * feature), low),
            jax.ShapeDtypeStruct((2 * lane, 2 * feature), low),
        ),
        in_specs=[VMEM] * 10,
        out_specs=(VMEM,) * 3,
        scratch_shapes=[
            pltpu.VMEM((feature, prompt_rows), low),
            pltpu.VMEM((feature, 2 * lane), low),
            pltpu.VMEM((prompt_rows, feature), low),
            pltpu.VMEM((2 * lane, feature), low),
            pltpu.VMEM((2, prompt_rows, feature), jnp.float32),
            pltpu.VMEM((2, 2 * lane, feature), jnp.float32),
            pltpu.VMEM((feature, lane), jnp.float32),
        ],
        compiler_params=pltpu.CompilerParams(vmem_limit_bytes=28 * MIB),
        cost_estimate=pl.CostEstimate(
            flops=20 * group * lane * total_rows * 128,
            bytes_accessed=12 * MIB,
            transcendentals=group * lane * total_rows,
        ),
    )(queries, far, near, *places, log_total, mixed, answer)


def head_places(back):
    n_z, n_x, n_c, n_y = sizes()
    line = n_z * n_c
    pairs = []
    for device in range(line * n_x * n_y):
        group, at = device // line, device % line
        place_of = ((at // n_c * n_x + group // n_y) * n_c + at % n_c) * n_y + group % n_y
        pairs.append((place_of, device) if back else (device, place_of))
    return tuple(pairs)


def pad_rows(block):
    return jnp.pad(block, ((0, 8 - block.shape[0]), (0, 0)))


def adam_update(weight, moment_one, moment_two, gradient, step_rate, decay_rate):
    first_new = BETA_ONE * moment_one + (1.0 - BETA_ONE) * gradient
    second_new = BETA_TWO * moment_two + (1.0 - BETA_TWO) * gradient * gradient
    normalized = (
        first_new
        / (1.0 - BETA_ONE**STEP)
        / (jnp.sqrt(second_new / (1.0 - BETA_TWO**STEP)) + ADAM_EPS)
    )
    return (weight - step_rate * (normalized + decay_rate * weight), first_new, second_new)


def per_device(
    token_ids,
    targets,
    valid_mask,
    cont_lengths,
    routes,
    vocab_table,
    vocab_first,
    vocab_second,
    attn_weights,
    attn_first,
    attn_second,
    router,
    router_first,
    router_second,
    norm_gains,
    gains_first,
    gains_second,
    expert_up,
    up_first,
    up_second,
    expert_down,
    down_first,
    down_second,
):
    slabs = lax.axis_size("z")
    planes = lax.axis_size("x")
    cores = lax.axis_size("core")
    sides = lax.axis_size("head")
    groups = planes * sides
    z_at, x_at, core_at, side_at = (lax.axis_index(name) for name in ALL)
    blk_at = (z_at * planes + x_at) * cores + core_at
    device_at = blk_at * sides + side_at
    group_at = x_at * sides + side_at
    tokens = valid_mask.shape[0]
    chunk = token_ids.shape[0]
    own = chunk // sides
    lane = planes * chunk
    feature = D // groups
    wide = expert_up.shape[3] // planes
    shard_rows = vocab_table.shape[0]
    logit_scale = D ** (-0.5)

    cont_ends = jnp.cumsum(cont_lengths)
    valid_f = valid_mask.astype(jnp.float32)
    token_count = jnp.sum(valid_mask).astype(jnp.float32)
    expert_ids = jnp.arange(EXPERTS, dtype=jnp.int32)

    own_ints = jnp.concatenate([token_ids[None], targets[None], routes], axis=0)
    own_ints = lax.dynamic_slice_in_dim(own_ints, side_at * own, own, axis=1).astype(jnp.float32)
    rows_of = attn_weights.shape[1]
    smalls = jnp.concatenate(
        [router.transpose(0, 2, 1).reshape(LAYERS * EXPERTS, rows_of), norm_gains], axis=0
    )
    smalls = smalls.astype(jnp.bfloat16).astype(jnp.float32)
    smalls = jnp.pad(smalls, ((0, 16 - smalls.shape[0]), (0, own - rows_of)))
    whole_f = swap(jnp.concatenate([pad_rows(own_ints), smalls], axis=0)[None], True, 1)
    attn_low = attn_weights.astype(jnp.bfloat16)
    qkv_send = attn_low[:, :, : 3 * D].reshape(LAYERS, rows_of, 3, groups, feature)
    qkv_send = jnp.concatenate([qkv_send[:, :, 1:], qkv_send[:, :, :1]], axis=2)
    qkv_send = qkv_send.transpose(3, 0, 1, 2, 4).reshape(groups, LAYERS, rows_of, 3 * feature)
    qkv_got = lax.all_to_all(qkv_send, PLANE, split_axis=0, concat_axis=0, tiled=True)
    out_rows = lax.ppermute(attn_low[:, :, 3 * D :], ALL, head_places(False))
    expert_send = jnp.stack([expert_up, expert_down], axis=1).astype(jnp.bfloat16)
    depth = expert_send.shape[3]
    expert_send = expert_send.reshape(LAYERS, 2 * EXPERTS, depth, planes, wide)
    expert_send = expert_send.transpose(3, 0, 1, 2, 4)
    expert_halves = []
    for layer_index in range(LAYERS):
        kept_half = lax.dynamic_index_in_dim(expert_send[:, layer_index], x_at, 0, False)
        sent_half = lax.dynamic_index_in_dim(expert_send[:, layer_index], 1 - x_at, 0, False)
        got_half = lax.ppermute(sent_half, "x", ((0, 1), (1, 0)))
        expert_halves.append((kept_half, got_half))
    got_halves = [got_half for _, got_half in expert_halves]
    whole_f, qkv_got, out_rows, got_halves = lax.optimization_barrier(
        (whole_f, qkv_got, out_rows, got_halves)
    )
    expert_halves = [(kept_half, got) for (kept_half, _), got in zip(expert_halves, got_halves)]
    qkv_own = qkv_got.reshape(planes, sides, LAYERS, rows_of, 3 * feature).transpose(2, 0, 1, 3, 4)
    qkv_own = qkv_own.reshape(LAYERS, planes, sides * rows_of, 3 * feature)

    def gather_experts(kept_half, got_half):
        if depth % 16 == 0:
            return lax.all_gather(kept_half, LINE, axis=0).reshape(
                (slabs, cores) + kept_half.shape
            ), lax.all_gather(got_half, LINE, axis=0).reshape((slabs, cores) + kept_half.shape)
        halves = jnp.stack(
            [jnp.where(x_at == 0, kept_half, got_half), jnp.where(x_at == 0, got_half, kept_half)]
        )
        block = lax.all_gather(halves, LINE, axis=0)
        block = block.reshape(slabs, cores, planes, 2 * EXPERTS, depth, wide)
        block = block.transpose(3, 0, 2, 1, 4, 5).reshape(1, 1, 2 * EXPERTS, D, wide)
        return block, block

    expert_weights = [gather_experts(*expert_halves[0])]
    ints = whole_f.reshape(sizes() + whole_f.shape[1:])
    whole = whole_f[:, : 2 + LAYERS].astype(jnp.int32)
    smalls = whole_f[:, 8:, :rows_of].transpose(1, 0, 2).reshape(16, D)
    router_all = smalls[: LAYERS * EXPERTS].reshape(LAYERS, EXPERTS, D).transpose(0, 2, 1)
    router_all = router_all.astype(jnp.bfloat16)
    gains_f = smalls[LAYERS * EXPERTS :]
    routes_lane = lax.dynamic_index_in_dim(
        whole.reshape(slabs, planes, cores, sides, 2 + LAYERS, own), z_at, 0, False
    )
    routes_lane = lax.dynamic_index_in_dim(routes_lane, core_at, 1, False)[:, :, 2:]
    routes_lane = routes_lane.transpose(2, 0, 1, 3)[..., None]
    routes_own = lax.dynamic_slice_in_dim(routes, side_at * own, own, axis=1)

    extent = -(-shard_rows // 256) * 256
    table = jnp.pad(vocab_table.astype(jnp.bfloat16), ((0, extent - shard_rows), (0, 0)))
    offsets = jnp.arange(chunk, dtype=jnp.int32)
    first_blk = z_at * planes * cores + core_at
    query_pos = jnp.concatenate([(first_blk + cores * part) * chunk + offsets for part in range(planes)])
    near_blks = [first_blk - 1 + part for part in range(2 * planes)]
    near_pos = jnp.concatenate([blk * chunk + offsets for blk in near_blks])
    query_seg = segment_of(query_pos, cont_ends)
    near_seg = segment_of(near_pos, cont_ends)
    places = (query_pos[None, :], query_seg[None, :], near_pos[None, :], near_seg[None, :])

    stream, qkv_all, out_all = embed(table, ints, qkv_own, out_rows, own, shard_rows, 2)
    qkv_weights = [qkv_all[layer_index].reshape(D, 3 * feature) for layer_index in range(LAYERS)]
    out_weights = [out_all[layer_index].reshape(feature, D) for layer_index in range(LAYERS)]

    kept = []
    for layer_index in range(LAYERS):
        normed_lane, key_values, queries = gather_project(
            rms_norm(stream, gains_f[2 * layer_index : 2 * layer_index + 1]).astype(jnp.bfloat16),
            qkv_weights[layer_index], False, (2 * feature, feature), None, 3,
        )
        queries = queries.reshape(lane, feature)
        far, near = spread_keys(key_values.reshape(lane, 2 * feature), PROMPT, 10)
        if layer_index + 1 < LAYERS:
            far, halves = lax.optimization_barrier((far, expert_halves[layer_index + 1]))
            expert_weights.append(gather_experts(*halves))
        mixed_t, mixed_low, log_total = attend(queries, far, near, places, chunk)
        (attended,) = project(
            mixed_low.reshape(planes, sides, own, feature), out_weights[layer_index], False, None, 15
        )
        middle = stream + attended
        normed_two = rms_norm(middle, gains_f[2 * layer_index + 1 : 2 * layer_index + 2]).astype(jnp.bfloat16)
        chance = jax.nn.softmax(matmul(normed_two, router_all[layer_index]), axis=-1)
        output, wide_rows, before, hidden = experts(
            normed_two, routes_lane[layer_index], expert_weights[layer_index], 11
        )
        own_pick = (routes_own[layer_index][:, None] == expert_ids[None, :]).astype(jnp.float32)
        gate = jnp.sum(chance * own_pick, axis=1, keepdims=True)
        kept.append(
            (
                stream, normed_lane, queries, far, near, mixed_t, mixed_low, log_total, middle,
                normed_two, chance, wide_rows, before, hidden, output, own_pick, gate,
            )
        )
        stream = middle + gate * output

    final_gain = gains_f[2 * LAYERS : 2 * LAYERS + 1]
    devices = tokens // own
    valid_rows = valid_f.reshape(sizes() + (1, own))
    final_all, row_logs, hits = gather_logits(
        rms_norm(stream, final_gain).astype(jnp.bfloat16), table, ints, valid_rows, shard_rows, 4
    )
    log_sums = merge_logs(row_logs.reshape(devices, 1, own), 5)
    log_sum = log_sums.reshape(tokens)
    own_log = lax.dynamic_slice_in_dim(log_sum, device_at * own, own)
    own_valid = lax.dynamic_slice_in_dim(valid_f, device_at * own, own)
    own_loss = jnp.sum(own_log * own_valid) - jnp.sum(hits)
    final_grad, table_grad = vocab_back(
        final_all, table, ints, log_sums.reshape(sizes() + (1, own)), valid_rows / token_count,
        shard_rows, 6,
    )
    stream_grad, final_gain_grad = jax.vjp(rms_norm, stream, final_gain)[1](final_grad)

    qkv_packs = [None] * LAYERS
    out_packs = [None] * LAYERS
    router_list = [None] * LAYERS
    expert_sums = [None] * LAYERS
    gain_list = [None] * (2 * LAYERS + 1)
    gain_list[2 * LAYERS] = final_gain_grad
    for layer_index in reversed(range(LAYERS)):
        (
            stream, normed_lane, queries, far, near, mixed_t, mixed_low, log_total, middle,
            normed_two, chance, wide_rows, before, hidden, output, own_pick, gate,
        ) = kept[layer_index]
        out_grad = (gate * stream_grad).astype(jnp.bfloat16)
        chance_grad = jnp.sum(stream_grad * output, axis=1)[:, None] * own_pick
        choice_grad = chance * (chance_grad - jnp.sum(chance * chance_grad, axis=1, keepdims=True))
        router_list[layer_index] = jnp.dot(
            normed_two.astype(jnp.float32).T, choice_grad, precision=lax.Precision.HIGHEST
        )
        normed_grad = jnp.dot(
            choice_grad,
            router_all[layer_index].astype(jnp.float32).T,
            precision=lax.Precision.HIGHEST,
        )
        rows_grad, expert_grad = experts_back(
            out_grad, routes_lane[layer_index], expert_weights[layer_index], wide_rows, before,
            hidden, 12,
        )
        normed_grad = normed_grad + rows_grad
        middle_part, gain_list[2 * layer_index + 1] = jax.vjp(
            rms_norm, middle, gains_f[2 * layer_index + 1 : 2 * layer_index + 2]
        )[1](normed_grad)
        middle_grad = stream_grad + middle_part
        _, answer, out_packs[layer_index] = gather_project(
            middle_grad.astype(jnp.bfloat16), out_weights[layer_index], True, (feature,), mixed_low, 16
        )
        answer = answer.reshape(lane, feature)
        query_grad, far_grad, near_grad = attend_back(
            queries, far, near, places, log_total, mixed_t, answer, chunk
        )
        qkv_grad = collect_keys(far_grad, near_grad, query_grad, 13)
        qkv_grad, expert_grad = lax.optimization_barrier((qkv_grad, expert_grad))
        expert_sums[layer_index] = lax.psum_scatter(
            expert_grad, LINE, scatter_dimension=0, tiled=True
        )[0]
        normed_att_grad, qkv_packs[layer_index] = project(
            qkv_grad.reshape(planes, sides, own, 3 * feature), qkv_weights[layer_index], True,
            normed_lane, 14,
        )
        stream_part, gain_list[2 * layer_index] = jax.vjp(
            rms_norm, stream, gains_f[2 * layer_index : 2 * layer_index + 1]
        )[1](normed_att_grad)
        stream_grad = middle_grad + stream_part

    small = jnp.concatenate(
        [jnp.stack(router_list).transpose(1, 0, 2).reshape(D, -1), jnp.concatenate(gain_list, axis=0).T], axis=1
    )
    small = small.reshape(devices, rows_of, -1).transpose(0, 2, 1)
    small = jnp.pad(small, ((0, 0), (0, 16 - small.shape[1]), (0, 128 - rows_of)))
    table_share, small, near_squares, *attn_sums = embed_back(
        stream_grad.astype(jnp.bfloat16), ints, table_grad, small, qkv_packs + out_packs, shard_rows, 7
    )
    squares = sum(
        jnp.sum(jnp.square(part.astype(jnp.float32)))
        for part in [small[:, :rows_of]] + expert_sums
    ) + jnp.sum(near_squares)
    sums = jnp.pad(jnp.stack([squares, own_loss])[:, None], ((0, 6), (0, 127)))
    sums = jnp.sum(swap(sums[None], True, 9)[:, :2, 0], axis=0)
    square_total, loss_sum = sums[0], sums[1]
    expert_shares = []
    for expert_grad in expert_sums:
        kept_half = lax.dynamic_index_in_dim(expert_grad, x_at, 0, False)
        sent_half = lax.dynamic_index_in_dim(expert_grad, 1 - x_at, 0, False)
        got_half = lax.ppermute(sent_half, "x", ((0, 1), (1, 0)))
        expert_grad = jnp.concatenate(
            [jnp.where(x_at == 0, kept_half, got_half), jnp.where(x_at == 0, got_half, kept_half)],
            axis=-1,
        )
        expert_shares.append(
            expert_grad.reshape(2, EXPERTS, depth, planes * wide).astype(jnp.float32)
        )
    table_share, small = table_share[:shard_rows], small[:, :rows_of]
    router_share = (
        small[: LAYERS * EXPERTS].reshape(LAYERS, EXPERTS, rows_of).transpose(0, 2, 1)
    )
    gain_share = small[LAYERS * EXPERTS : LAYERS * EXPERTS + 2 * LAYERS + 1]
    qkv_share = jnp.stack(attn_sums[:LAYERS], axis=1).reshape(
        planes, LAYERS, sides, rows_of, 3 * feature
    )
    qkv_share = qkv_share.transpose(0, 2, 1, 3, 4).reshape(groups, LAYERS, rows_of, 3 * feature)
    qkv_share = lax.all_to_all(qkv_share, PLANE, split_axis=0, concat_axis=0, tiled=True)
    qkv_share = qkv_share.reshape(groups, LAYERS, rows_of, 3, feature)
    qkv_share = jnp.concatenate([qkv_share[:, :, :, 2:], qkv_share[:, :, :, :2]], axis=3)
    qkv_share = qkv_share.transpose(1, 2, 3, 0, 4).reshape(LAYERS, rows_of, 3 * D)
    out_share = lax.ppermute(jnp.stack(attn_sums[LAYERS:]), ALL, head_places(True))
    attn_share = jnp.concatenate([qkv_share, out_share], axis=2).astype(jnp.float32)
    up_share = jnp.stack([share[0] for share in expert_shares])
    down_share = jnp.stack([share[1] for share in expert_shares])
    shares = (table_share, attn_share, router_share, gain_share, up_share, down_share)
    grad_norm = jnp.sqrt(square_total)
    factor = CLIP_AT / jnp.maximum(grad_norm, CLIP_AT)
    weights = (vocab_table, attn_weights, router, norm_gains, expert_up, expert_down)
    firsts = (vocab_first, attn_first, router_first, gains_first, up_first, down_first)
    seconds = (vocab_second, attn_second, router_second, gains_second, up_second, down_second)
    results = [loss_sum, token_count, grad_norm]
    for number in range(6):
        results.extend(
            adam_update(
                weights[number],
                firsts[number],
                seconds[number],
                factor * shares[number],
                STEP_RATES[number],
                DECAY_RATES[number],
            )
        )
    return tuple(results)


def solution(mesh):
    blocks, sides = mesh.shape["blk"], mesh.shape["head"]
    fine = Mesh(mesh.devices.reshape(blocks // 4, 2, 2, sides), ALL)
    weight_specs = (
        (P(ALL, None),) * 3
        + (P(None, ALL, None),) * 3
        + (P(None, ALL, None),) * 3
        + (P(None, ALL),) * 3
        + (P(None, None, BLK, "head"),) * 6
    )
    return jax.shard_map(
        per_device,
        mesh=fine,
        in_specs=(P(BLK), P(BLK), P(), P(), P(None, BLK)) + weight_specs,
        out_specs=(P(), P(), P()) + weight_specs,
        check_vma=False,
    )
```

profile of v0, /device:TPU:0, one launch (start us, length us, event | category | flops | bytes accessed | tf_op | source)
XLA Modules:
  0.0 746.7 jit_solution(9899366020541382594)
XLA Ops:
  31.4 20.3 %shard_map.382 = f32[32,24,128]{2,1,0:T(8,128)S(1)} custom-call(f32[1,24,128]{2,1,0:T(8,128)S(1)} %fusion.11.source), custom_call_target="tpu_custom_call" | custom-call | bytes 37748736 | tf_op jit(solution)/shard_map/pallas_call | solution.py:123
  57.2 59.8 %shard_map.383 = (f32[128,768]{1,0:T(8,128)S(1)}, bf16[2,4,2,2,48,576]{5,4,3,2,1,0:T(8,128)(2,1)S(1)}, bf16[2,4,2,24,768]{4,3,2,1,0:T(8,128)(2,1)S(1)}) custom-call(bf16[1024,768]{1,0:T(8,128)(2,1)S(1)} %pad.23.table, f32[4,2,2,2,24,128]{5,4,3,2,1,0:T(8,128)S(1)} %bitcast.157, bf16[2,2,48,576]{3,2,1,0:T(8,128)(2,1)S(1)} %bitcast.179, ...), custom_call_target="tpu_custom_call" | custom-call | bytes 125829120 | tf_op jit(solution)/shard_map/pallas_call | solution.py:1307
  119.0 10.9 %shard_map.384 = (bf16[2,2,128,768]{3,2,1,0:T(8,128)(2,1)S(1)}, bf16[2,2,128,384]{3,2,1,0:T(8,128)(2,1)S(1)}, bf16[2,2,128,192]{3,2,1,0:T(8,128)(2,1)S(1)}) custom-call(bf16[128,768]{1,0:T(8,128)(2,1)S(1)} %multiply_convert_fusion.6.own_rows, bf16[768,576]{1,0:T(8,128)(2,1)S(1)} %bitcast.161), custom_call_target="tpu_custom_call" | custom-call | flops 452984832 | bytes 25165824 | tf_op jit(solution)/shard_map/pallas_call | solution.py:1814
  131.5 12.5 %shard_map.385 = (bf16[2,2,512,384]{3,2,1,0:T(8,128)(2,1)S(1)}, bf16[4,256,384]{2,1,0:T(8,128)(2,1)S(1)}, bf16[256,384]{1,0:T(8,128)(2,1)}) custom-call(bf16[512,384]{1,0:T(8,128)(2,1)S(1)} %bitcast.182), custom_call_target="tpu_custom_call" | custom-call | bytes 62914560 | tf_op jit(solution)/shard_map/pallas_call | solution.py:334
  159.2 10.5 %shard_map.386 = (f32[192,512]{1,0:T(8,128)S(1)}, bf16[512,192]{1,0:T(8,128)(2,1)S(1)}, f32[3,512]{1,0:T(4,128)S(1)}) custom-call(bf16[512,192]{1,0:T(8,128)(2,1)S(1)} %bitcast.217, bf16[2048,384]{1,0:T(8,128)(2,1)S(1)} %bitcast.207, bf16[1024,384]{1,0:T(8,128)(2,1)S(1)} %bitcast.211, s32[1,512]{1,0:T(1,128)S(1)} %bitcast.195, ...), custom_call_target="tpu_custom_call" | custom-call | flops 4026531840 | bytes 8388608 | tf_op jit(solution)/shard_map/pallas_call | solution.py:2003
  170.7 12.4 %shard_map.387 = f32[128,768]{1,0:T(8,128)S(1)} custom-call(bf16[2,2,128,192]{3,2,1,0:T(8,128)(2,1)S(1)} %bitcast.173, bf16[192,768]{1,0:T(8,128)(2,1)S(1)} %bitcast.165), custom_call_target="tpu_custom_call" | custom-call | flops 150994944 | bytes 25165824 | tf_op jit(solution)/shard_map/pallas_call | solution.py:1747
  189.8 20.9 %shard_map.388 = (f32[128,768]{1,0:T(8,128)S(1)}, bf16[2,2,128,768]{3,2,1,0:T(8,128)(2,1)S(1)}, f32[2,2,128,768]{3,2,1,0:T(8,128)S(1)}, bf16[2,2,128,768]{3,2,1,0:T(8,128)(2,1)S(1)}) custom-call(bf16[128,768]{1,0:T(8,128)(2,1)S(1)} %multiply_convert_fusion.5.own_rows, s32[2,2,128,1]{3,2,1,0:T(8,128)S(1)} %copy-done.33, ...), custom_call_target="tpu_custom_call" | custom-call | flops 2415919104 | bytes 56623104 | tf_op jit(solution)/shard_map/pallas_call | solution.py:1556
  223.5 21.9 %shard_map.390 = (bf16[2,2,512,384]{3,2,1,0:T(8,128)(2,1)S(1)}, bf16[4,256,384]{2,1,0:T(8,128)(2,1)S(1)}, bf16[256,384]{1,0:T(8,128)(2,1)}) custom-call(bf16[512,384]{1,0:T(8,128)(2,1)S(1)} %bitcast.183), custom_call_target="tpu_custom_call" | custom-call | bytes 62914560 | tf_op jit(solution)/shard_map/pallas_call | solution.py:334
  245.5 10.5 %shard_map.391 = (f32[192,512]{1,0:T(8,128)S(1)}, bf16[512,192]{1,0:T(8,128)(2,1)S(1)}, f32[3,512]{1,0:T(4,128)S(1)}) custom-call(bf16[512,192]{1,0:T(8,128)(2,1)S(1)} %bitcast.219, bf16[2048,384]{1,0:T(8,128)(2,1)S(1)} %bitcast.209, bf16[1024,384]{1,0:T(8,128)(2,1)S(1)} %bitcast.213, s32[1,512]{1,0:T(1,128)S(1)} %bitcast.196, s32[1,512]{1,0:T(1,128)S(1)} %copy-done.48, ...), custom_call_target="tpu_custom_call" | custom-call | flops 4026531840 | bytes 8388608 | tf_op jit(solution)/shard_map/pallas_call | solution.py:2003
  256.1 12.7 %shard_map.392 = f32[128,768]{1,0:T(8,128)S(1)} custom-call(bf16[2,2,128,192]{3,2,1,0:T(8,128)(2,1)S(1)} %bitcast.174, bf16[192,768]{1,0:T(8,128)(2,1)S(1)} %bitcast.167), custom_call_target="tpu_custom_call" | custom-call | flops 150994944 | bytes 25165824 | tf_op jit(solution)/shard_map/pallas_call | solution.py:1747
  275.8 20.5 %shard_map.393 = (f32[128,768]{1,0:T(8,128)S(1)}, bf16[2,2,128,768]{3,2,1,0:T(8,128)(2,1)S(1)}, f32[2,2,128,768]{3,2,1,0:T(8,128)S(1)}, bf16[2,2,128,768]{3,2,1,0:T(8,128)(2,1)S(1)}) custom-call(bf16[128,768]{1,0:T(8,128)(2,1)S(1)} %multiply_convert_fusion.3.own_rows, s32[2,2,128,1]{3,2,1,0:T(8,128)S(1)} %copy-done.35, ...), custom_call_target="tpu_custom_call" | custom-call | flops 2415919104 | bytes 56623104 | tf_op jit(solution)/shard_map/pallas_call | solution.py:1556
  297.1 49.8 %shard_map.394 = (bf16[4,2,2,2,128,768]{5,4,3,2,1,0:T(8,128)(2,1)S(1)}, f32[4,2,2,2,1,128]{5,4,3,2,1,0:T(1,128)S(1)}, f32[1,256]{1,0:T(1,128)S(1)}) custom-call(bf16[128,768]{1,0:T(8,128)(2,1)S(1)} %multiply_convert_fusion.2.rows_in, bf16[1024,768]{1,0:T(8,128)(2,1)S(1)} %pad.23.table, f32[4,2,2,2,24,128]{5,4,3,2,1,0:T(8,128)S(1)} %bitcast.158, ...), custom_call_target="tpu_custom_call" | custom-call | bytes 113246208 | tf_op jit(solution)/shard_map/pallas_call | solution.py:968
  347.0 18.1 %shard_map.395 = f32[32,1,128]{2,1,0:T(1,128)S(1)} custom-call(f32[32,1,128]{2,1,0:T(1,128)S(1)} %bitcast.190), custom_call_target="tpu_custom_call" | custom-call | bytes 44040192 | tf_op jit(solution)/shard_map/pallas_call | solution.py:1888
  365.1 50.2 %shard_map.396 = (f32[128,768]{1,0:T(8,128)S(1)}, f32[1024,768]{1,0:T(8,128)S(1)}) custom-call(bf16[4,2,2,2,128,768]{5,4,3,2,1,0:T(8,128)(2,1)S(1)} %get-tuple-element.113.rows_all, bf16[1024,768]{1,0:T(8,128)(2,1)S(1)} %pad.23.table, f32[4,2,2,2,24,128]{5,4,3,2,1,0:T(8,128)S(1)} %bitcast.159, f32[4,2,2,2,1,128]{5,4,3,2,1,0:T(1,128)S(1)} %bitcast.188, ...), custom_call_target="tpu_custom_call" | custom-call | bytes 150994944 | tf_op jit(solution)/shard_map/pallas_call | solution.py:1382
  418.7 18.8 %shard_map.397 = (f32[128,768]{1,0:T(8,128)S(1)}, bf16[8,2,4,48,768]{4,3,2,1,0:T(8,128)(2,1)S(1)}) custom-call(bf16[128,768]{1,0:T(8,128)(2,1)S(1)} %multiply_convert_fusion.1.own_rows, s32[2,2,128,1]{3,2,1,0:T(8,128)S(1)} %copy-done.36, bf16[4,2,4,48,768]{4,3,2,1,0:T(8,128)(2,1)S(1)} %bitcast.204, bf16[4,2,4,48,768]{4,3,2,1,0:T(8,128)(2,1)S(1)} %bitcast.206, ...), custom_call_target="tpu_custom_call" | custom-call | flops 4831838208 | bytes 56623104 | tf_op jit(solution)/shard_map/pallas_call | solution.py:1668
  441.3 9.7 %shard_map.398 = (bf16[2,2,128,768]{3,2,1,0:T(8,128)(2,1)}, bf16[2,2,128,192]{3,2,1,0:T(8,128)(2,1)S(1)}, bf16[2,4,24,768]{3,2,1,0:T(8,128)(2,1)S(1)}) custom-call(bf16[128,768]{1,0:T(8,128)(2,1)S(1)} %get-tuple-element.196.own_rows, bf16[192,768]{1,0:T(8,128)(2,1)S(1)} %bitcast.168, bf16[512,192]{1,0:T(8,128)(2,1)S(1)} %copy-done.20), custom_call_target="tpu_custom_call" | custom-call | flops 150994944 | bytes 25165824 | tf_op jit(solution)/shard_map/pallas_call | solution.py:1814
  451.8 15.1 %shard_map.399 = (bf16[512,192]{1,0:T(8,128)(2,1)S(1)}, bf16[2048,384]{1,0:T(8,128)(2,1)S(1)}, bf16[1024,384]{1,0:T(8,128)(2,1)S(1)}) custom-call(bf16[512,192]{1,0:T(8,128)(2,1)S(1)} %bitcast.220, bf16[2048,384]{1,0:T(8,128)(2,1)S(1)} %bitcast.210, bf16[1024,384]{1,0:T(8,128)(2,1)S(1)} %bitcast.214, s32[1,512]{1,0:T(1,128)S(1)} %bitcast.197, ...), custom_call_target="tpu_custom_call" | custom-call | flops 10066329600 | bytes 12582912 | tf_op jit(solution)/shard_map/pallas_call | solution.py:2110
  466.8 20.8 %shard_map.400 = bf16[512,576]{1,0:T(8,128)(2,1)S(1)} custom-call(bf16[2,2,512,384]{3,2,1,0:T(8,128)(2,1)S(1)} %bitcast.172, bf16[4,256,384]{2,1,0:T(8,128)(2,1)S(1)} %bitcast.181, bf16[512,192]{1,0:T(8,128)(2,1)S(1)} %get-tuple-element.125.query_grad), custom_call_target="tpu_custom_call" | custom-call | bytes 62914560 | tf_op jit(solution)/shard_map/pallas_call | solution.py:496
  505.6 19.2 %shard_map.402 = (f32[128,768]{1,0:T(8,128)S(1)}, bf16[8,2,4,48,768]{4,3,2,1,0:T(8,128)(2,1)S(1)}) custom-call(bf16[128,768]{1,0:T(8,128)(2,1)S(1)} %multiply_convert_fusion.own_rows, s32[2,2,128,1]{3,2,1,0:T(8,128)S(1)} %copy-done.34, bf16[4,2,4,48,768]{4,3,2,1,0:T(8,128)(2,1)S(1)} %bitcast.200, bf16[4,2,4,48,768]{4,3,2,1,0:T(8,128)(2,1)S(1)} %bitcast.202, ...), custom_call_target="tpu_custom_call" | custom-call | flops 4831838208 | bytes 56623104 | tf_op jit(solution)/shard_map/pallas_call | solution.py:1668
  528.7 10.7 %shard_map.403 = (bf16[2,2,128,768]{3,2,1,0:T(8,128)(2,1)}, bf16[2,2,128,192]{3,2,1,0:T(8,128)(2,1)S(1)}, bf16[2,4,24,768]{3,2,1,0:T(8,128)(2,1)S(1)}) custom-call(bf16[128,768]{1,0:T(8,128)(2,1)S(1)} %get-tuple-element.192.own_rows, bf16[192,768]{1,0:T(8,128)(2,1)S(1)} %bitcast.166, bf16[512,192]{1,0:T(8,128)(2,1)S(1)} %copy-done.18), custom_call_target="tpu_custom_call" | custom-call | flops 150994944 | bytes 25165824 | tf_op jit(solution)/shard_map/pallas_call | solution.py:1814
  539.4 15.0 %shard_map.404 = (bf16[512,192]{1,0:T(8,128)(2,1)S(1)}, bf16[2048,384]{1,0:T(8,128)(2,1)S(1)}, bf16[1024,384]{1,0:T(8,128)(2,1)S(1)}) custom-call(bf16[512,192]{1,0:T(8,128)(2,1)S(1)} %bitcast.218, bf16[2048,384]{1,0:T(8,128)(2,1)S(1)} %bitcast.208, bf16[1024,384]{1,0:T(8,128)(2,1)S(1)} %bitcast.212, s32[1,512]{1,0:T(1,128)S(1)} %bitcast.198, ...), custom_call_target="tpu_custom_call" | custom-call | flops 10066329600 | bytes 12582912 | tf_op jit(solution)/shard_map/pallas_call | solution.py:2110
  554.5 30.9 %shard_map.405 = bf16[512,576]{1,0:T(8,128)(2,1)S(1)} custom-call(bf16[2,2,512,384]{3,2,1,0:T(8,128)(2,1)S(1)} %bitcast.171, bf16[4,256,384]{2,1,0:T(8,128)(2,1)S(1)} %bitcast.180, bf16[512,192]{1,0:T(8,128)(2,1)S(1)} %get-tuple-element.139.query_grad), custom_call_target="tpu_custom_call" | custom-call | bytes 62914560 | tf_op jit(solution)/shard_map/pallas_call | solution.py:496
  601.6 71.1 %shard_map.407 = (f32[1024,768]{1,0:T(8,128)S(1)}, f32[16,128]{1,0:T(8,128)S(1)}, f32[1,768]{1,0:T(1,128)S(1)}, f32[2,48,576]{2,1,0:T(8,128)S(1)}, f32[2,48,576]...) custom-call(bf16[128,768]{1,0:T(8,128)(2,1)S(1)} %fusion.9.rows_in, ...), custom_call_target="tpu_custom_call" | custom-call | bytes 125829120 | tf_op jit(solution)/shard_map/pallas_call | solution.py:1043
  699.7 14.5 %shard_map.408 = f32[32,8,128]{2,1,0:T(8,128)S(1)} custom-call(f32[1,8,128]{2,1,0:T(8,128)S(1)} %pad_bitcast_fusion.source), custom_call_target="tpu_custom_call" | custom-call | bytes 37748736 | tf_op jit(solution)/shard_map/pallas_call | solution.py:123
  (515 shorter events, 165.6 us)
Async XLA Ops:
  7.2 178.4 %all-gather.9.cloned.1.call-start = ((), (), s32[]{:S(2)}) async-start(), calls=%async_computation.6 | async-start | bytes 2654208 | tf_op jit(solution)/shard_map/all_gather | solution.py:2246
  16.4 35.3 %collective-permute-start = (bf16[2,24,768]{2,1,0:T(8,128)(2,1)S(1)}, bf16[2,24,768]{2,1,0:T(8,128)(2,1)S(1)}, u32[]{:S(2)}, u32[]{:S(2)}) collective-permute-start(bf16[2,24,768]{2,1,0:T(8,128)(2,1)S(1)} %slice.208), channel_id=1, source_target_pairs={{0,0},{1,2},{2,8},{3,10},{4,16},{5,18},{6,24},{7,26},{8,1},{9,3},{... | collective-permute-start | bytes 221192 | tf_op jit(solution)/shard_map/ppermute | solution.py:2225
  19.3 32.4 %all-to-all-start = ((bf16[4,2,24,576]{3,2,1,0:T(8,128)(2,1)}), bf16[4,2,24,576]{3,2,1,0:T(8,128)(2,1)S(1)}, u32[]{:S(2)}, u32[]{:S(2)}) async-start(bf16[4,2,24,576]{3,2,1,0:T(8,128)(2,1)} %reshape.483), calls=%async_computation | async-start | bytes 491520 | tf_op jit(solution)/shard_map/all_to_all | solution.py:2224
  27.7 157.9 %all-gather.11.cloned.1.call-start = ((), (), s32[]{:S(2)}) async-start(), calls=%async_computation.7 | async-start | bytes 2654208 | tf_op jit(solution)/shard_map/all_gather | solution.py:2248
  29.0 22.7 %collective-permute-start.2 = (bf16[4,48,768]{2,1,0:T(8,128)(2,1)S(1)}, bf16[4,48,768]{2,1,0:T(8,128)(2,1)S(1)}, u32[]{:S(2)}, u32[]{:S(2)}) collective-permute-start(bf16[4,48,768]{2,1,0:T(8,128)(2,1)S(1)} %bitcast.224), channel_id=1, source_target_pairs={{0,4},{4,0},{1,5},{5,1},{2,6},{6,2},{3,7},{7,3},{8,12},{12,8},{9,1... | collective-permute-start | bytes 884744 | tf_op jit(solution)/shard_map/ppermute | solution.py:2234
  31.1 20.6 %collective-permute-start.1 = (bf16[4,48,768]{2,1,0:T(8,128)(2,1)S(1)}, bf16[4,48,768]{2,1,0:T(8,128)(2,1)S(1)}, u32[]{:S(2)}, u32[]{:S(2)}) collective-permute-start(bf16[4,48,768]{2,1,0:T(8,128)(2,1)S(1)} %bitcast.225), channel_id=1, source_target_pairs={{0,4},{4,0},{1,5},{5,1},{2,6},{6,2},{3,7},{7,3},{8,12},{12,8},{9,1... | collective-permute-start | bytes 884744 | tf_op jit(solution)/shard_map/ppermute | solution.py:2234
  52.6 218.9 %all-gather.13.cloned.1.call-start = ((), (), s32[]{:S(2)}) async-start(), calls=%async_computation.8 | async-start | bytes 2654208 | tf_op jit(solution)/shard_map/all_gather | solution.py:2246
  56.9 60.3 %copy-start.111 = (f32[768]{0:T(1024)}, f32[768]{0:T(1024)S(1)}, u32[]{:S(2)}) copy-start(f32[768]{0:T(1024)S(1)} %mul.648) | copy-start | bytes 9220
  146.0 125.5 %all-gather.15.cloned.1.call-start = ((), (), s32[]{:S(2)}) async-start(), calls=%async_computation.9 | async-start | bytes 2654208 | tf_op jit(solution)/shard_map/all_gather | solution.py:2248
  155.2 533.6 %reduce-scatter.5.cloned.1.call-start = ((), (), s32[]{:S(2)}) async-start(), calls=%async_computation.5 | async-start | bytes 5308416 | tf_op jit(solution)/shard_map/reduce_scatter | solution.py:2374
  211.9 33.5 %copy-start.156 = (f32[128]{0:T(128)}, f32[128]{0:T(128)S(1)}, u32[]{:S(2)}) copy-start(f32[128]{0:T(128)S(1)} %get-tuple-element.206) | copy-start | bytes 1540
  211.9 56.9 %copy-start.90 = (f32[128,768]{1,0:T(8,128)}, f32[128,768]{1,0:T(8,128)S(1)}, u32[]{:S(2)}) copy-start(f32[128,768]{1,0:T(8,128)S(1)} %get-tuple-element.207) | copy-start | bytes 1179652
  211.9 33.5 %copy-start.144 = (f32[128]{0:T(128)}, f32[128]{0:T(128)S(1)}, u32[]{:S(2)}) copy-start(f32[128]{0:T(128)S(1)} %fusion.36) | copy-start | bytes 1540
  212.4 33.0 %copy-start.39 = (s32[1024]{0:T(1024)S(1)}, s32[1024]{0:T(1024)}, u32[]{:S(2)}) copy-start(s32[1024]{0:T(1024)} %copy-done.38) | copy-start | bytes 12292
  212.5 33.0 %copy-start.42 = (s32[1,1024]{1,0:T(1,128)S(1)}, s32[1,1024]{1,0:T(1,128)}, u32[]{:S(2)}) copy-start(s32[1,1024]{1,0:T(1,128)} %copy-done.41) | copy-start | bytes 12292
  212.5 33.0 %copy-start.45 = (s32[512]{0:T(512)S(1)}, s32[512]{0:T(512)}, u32[]{:S(2)}) copy-start(s32[512]{0:T(512)} %copy-done.44) | copy-start | bytes 6148
  212.5 33.0 %copy-start.48 = (s32[1,512]{1,0:T(1,128)S(1)}, s32[1,512]{1,0:T(1,128)}, u32[]{:S(2)}) copy-start(s32[1,512]{1,0:T(1,128)} %copy-done.47) | copy-start | bytes 6148
  297.1 67.9 %copy-start.37 = (f32[4,2,2,2,1,128]{5,4,3,2,1,0:T(1,128)S(1)}, f32[4,2,2,2,1,128]{5,4,3,2,1,0:T(1,128)}, u32[]{:S(2)}) copy-start(f32[4,2,2,2,1,128]{5,4,3,2,1,0:T(1,128)} %broadcast_divide_fusion.weights) | copy-start | bytes 49156
  365.1 53.0 %copy-start.57 = (bf16[32,48,768]{2,1,0:T(8,128)(2,1)S(1)}, bf16[32,48,768]{2,1,0:T(8,128)(2,1)}, u32[]{:S(2)}) copy-start(bf16[32,48,768]{2,1,0:T(8,128)(2,1)} %all-gather.15.cloned.1.call-done) | copy-start | bytes 7077892
  487.7 206.3 %reduce-scatter.3.cloned.1.call-start = ((), (), s32[]{:S(2)}) async-start(), calls=%async_computation.4 | async-start | bytes 5308416 | tf_op jit(solution)/shard_map/reduce_scatter | solution.py:2374
  675.3 11.6 %all-to-all-start.1 = ((f32[4,2,24,576]{3,2,1,0:T(8,128)}), f32[4,2,24,576]{3,2,1,0:T(8,128)S(1)}, u32[]{:S(2)}, u32[]{:S(2)}) async-start(f32[4,2,24,576]{3,2,1,0:T(8,128)} %bitcast.76), calls=%async_computation.3 | async-start | bytes 983040 | tf_op jit(solution)/shard_map/all_to_all | solution.py:2422
  680.5 45.8 %collective-permute-start.3 = (f32[2,24,768]{2,1,0:T(8,128)S(1)}, f32[2,24,768]{2,1,0:T(8,128)S(1)}, u32[]{:S(2)}, u32[]{:S(2)}) collective-permute-start(f32[2,24,768]{2,1,0:T(8,128)S(1)} %pad_maximum_fusion.2), channel_id=1, source_target_pairs={{0,0},{2,1},{8,2},{10,3},{16,4},{18,5},{24,6},{26,7},{1,8},{3,9},{... | collective-permute-start | bytes 442376 | tf_op jit(solution)/shard_map/ppermute | solution.py:2426
  689.9 39.2 %collective-permute-start.5 = (bf16[4,48,768]{2,1,0:T(8,128)(2,1)S(1)}, bf16[4,48,768]{2,1,0:T(8,128)(2,1)S(1)}, u32[]{:S(2)}, u32[]{:S(2)}) collective-permute-start(bf16[4,48,768]{2,1,0:T(8,128)(2,1)S(1)} %dynamic-slice_bitcast_fusion), channel_id=1, source_target_pairs={{0,4},{4,0},{1,5},{5,1},{2,6},{6,2},{3,7},{7,3},{8,12},{12,8},{9,1... | collective-permute-start | bytes 884744 | tf_op jit(solution)/shard_map/ppermute | solution.py:2405
  715.7 13.7 %collective-permute-start.4 = (bf16[4,48,768]{2,1,0:T(8,128)(2,1)S(1)}, bf16[4,48,768]{2,1,0:T(8,128)(2,1)S(1)}, u32[]{:S(2)}, u32[]{:S(2)}) collective-permute-start(bf16[4,48,768]{2,1,0:T(8,128)(2,1)S(1)} %dynamic-slice_bitcast_fusion.1), channel_id=1, source_target_pairs={{0,4},{4,0},{1,5},{5,1},{2,6},{6,2},{3,7},{7,3},{8,12},{12,8},{9,1... | collective-permute-start | bytes 884744 | tf_op jit(solution)/shard_map/ppermute | solution.py:2405
  (151 other events, 1098.1 us)
Sparse Core Ops, SparseCore 0:
  16.1 42.8 all-gather.8
  61.3 39.1 all-gather.10
  146.1 44.7 all-gather.12
  192.4 31.1 all-gather.14
  487.8 58.1 reduce-scatter.4
  585.5 88.5 reduce-scatter.2
where the time goes:
time: 754 us; the launch traced here: 747 us
  Pallas kernels  583 us (77%)
  local copies, waits for them, and re-layouts  73.5 us (10%)
  other arithmetic  37.8 us (5%)
  between operations  24.5 us (3%)
  starting transfers between devices  22.8 us (3%)
    pallas_call x1, Pallas kernels, embed_back(): pl.pallas_call(functools.partial(embed_back_kernel, shard_rows, len(packs...  71.1 us
    pallas_call x1, Pallas kernels, embed(): pl.pallas_call(functools.partial(embed_kernel, shard_rows), out_shape=(ja...  59.8 us
    pallas_call x2, Pallas kernels, collect_keys(): pl.pallas_call(functools.partial(collect_kernel, slabs), out_shape=jax.Sh...  51.6 us
    pallas_call x1, Pallas kernels, vocab_back(): pl.pallas_call(functools.partial(vocab_back_kernel, shard_rows, held), ou...  50.2 us
    pallas_call x1, Pallas kernels, gather_logits(): pl.pallas_call(functools.partial(logits_kernel, shard_rows), out_shape=(j...  49.8 us
    unnamed x327, local copies, waits for them, and re-layouts  49.4 us
    pallas_call x4, Pallas kernels, project(): pl.pallas_call(functools.partial(project_kernel, transposed, left is not...  42.8 us
    pallas_call x2, Pallas kernels, experts(): pl.pallas_call(experts_kernel, out_shape=(jax.ShapeDtypeStruct((own, widt...  41.4 us
  transfers between devices with their start and end apart: 14, of which 1 were waited for; matrix products, arithmetic and copies ran while one was open for 7% of the time, Pallas kernels for 51%

commit v1 on v0

--- a/solution.py
+++ b/solution.py
@@ -1570,7 +1570,7 @@
             dma((width // weights[0].shape[3],)), dma((6,)), dma((6,)), dma((3,)), dma((3,)),
         ],
         compiler_params=pltpu.CompilerParams(
-            collective_id=collective_id, has_side_effects=True, vmem_limit_bytes=20 * MIB
+            collective_id=collective_id, has_side_effects=True, vmem_limit_bytes=56 * MIB
         ),
         cost_estimate=pl.CostEstimate(
             flops=8 * own * 4 * width * wide, bytes_accessed=54 * MIB, transcendentals=4 * own * wide
@@ -1685,7 +1685,7 @@
             dma((width // weights[0].shape[3],)), dma((3,)), dma((4,)), dma((6,)), dma((6,)), dma((3,)), dma((3,)),
         ],
         compiler_params=pltpu.CompilerParams(
-            collective_id=collective_id, has_side_effects=True, vmem_limit_bytes=34 * MIB
+            collective_id=collective_id, has_side_effects=True, vmem_limit_bytes=56 * MIB
         ),
         cost_estimate=pl.CostEstimate(
             flops=16 * own * 4 * width * units, bytes_accessed=54 * MIB, transcendentals=8 * own * units
@@ -2231,13 +2231,15 @@
     for layer_index in range(LAYERS):
         kept_half = lax.dynamic_index_in_dim(expert_send[:, layer_index], x_at, 0, False)
         sent_half = lax.dynamic_index_in_dim(expert_send[:, layer_index], 1 - x_at, 0, False)
-        got_half = lax.ppermute(sent_half, "x", ((0, 1), (1, 0)))
-        expert_halves.append((kept_half, got_half))
-    got_halves = [got_half for _, got_half in expert_halves]
-    whole_f, qkv_got, out_rows, got_halves = lax.optimization_barrier(
-        (whole_f, qkv_got, out_rows, got_halves)
+        expert_halves.append((kept_half, sent_half))
+
+    def across(half):
+        return lax.ppermute(half, "x", ((0, 1), (1, 0)))
+
+    got_half = across(expert_halves[0][1])
+    whole_f, qkv_got, out_rows, got_half = lax.optimization_barrier(
+        (whole_f, qkv_got, out_rows, got_half)
     )
-    expert_halves = [(kept_half, got) for (kept_half, _), got in zip(expert_halves, got_halves)]
     qkv_own = qkv_got.reshape(planes, sides, LAYERS, rows_of, 3 * feature).transpose(2, 0, 1, 3, 4)
     qkv_own = qkv_own.reshape(LAYERS, planes, sides * rows_of, 3 * feature)
 
@@ -2254,7 +2256,7 @@
         block = block.transpose(3, 0, 2, 1, 4, 5).reshape(1, 1, 2 * EXPERTS, D, wide)
         return block, block
 
-    expert_weights = [gather_experts(*expert_halves[0])]
+    expert_weights = [gather_experts(expert_halves[0][0], got_half)]
     ints = whole_f.reshape(sizes() + whole_f.shape[1:])
     whole = whole_f[:, : 2 + LAYERS].astype(jnp.int32)
     smalls = whole_f[:, 8:, :rows_of].transpose(1, 0, 2).reshape(16, D)
@@ -2289,11 +2291,15 @@
             rms_norm(stream, gains_f[2 * layer_index : 2 * layer_index + 1]).astype(jnp.bfloat16),
             qkv_weights[layer_index], False, (2 * feature, feature), None, 3,
         )
+        if layer_index + 1 < LAYERS:
+            kept_half, sent_half = expert_halves[layer_index + 1]
+            key_values, sent_half = lax.optimization_barrier((key_values, sent_half))
+            got_half = across(sent_half)
         queries = queries.reshape(lane, feature)
         far, near = spread_keys(key_values.reshape(lane, 2 * feature), PROMPT, 10)
         if layer_index + 1 < LAYERS:
-            far, halves = lax.optimization_barrier((far, expert_halves[layer_index + 1]))
-            expert_weights.append(gather_experts(*halves))
+            far, kept_half, got_half = lax.optimization_barrier((far, kept_half, got_half))
+            expert_weights.append(gather_experts(kept_half, got_half))
         mixed_t, mixed_low, log_total = attend(queries, far, near, places, chunk)
         (attended,) = project(
             mixed_low.reshape(planes, sides, own, feature), out_weights[layer_index], False, None, 15

time: 754 us -> 736 us (0.976)
  local copies, waits for them, and re-layouts: 73.5 us -> 53.1 us
    unnamed x327 -> x189, local copies, waits for them, and re-layouts: 49.4 us -> 31.5 us
  transfers between devices with their start and end apart: 14 -> 14, of which waited for: 1 -> 1; matrix products, arithmetic and copies ran while one was open for 7% -> 7% of each run, Pallas kernels for 51% -> 52%
where the time goes in v1:
time: 736 us; the launch traced here: 727 us
  Pallas kernels  585 us (79%)
  local copies, waits for them, and re-layouts  53.1 us (7%)
  other arithmetic  36.4 us (5%)
  starting transfers between devices  24.5 us (3%)
  between operations  23.6 us (3%)
    pallas_call x1, Pallas kernels, embed_back(): pl.pallas_call(functools.partial(embed_back_kernel, shard_rows, len(packs...  71.1 us
    pallas_call x1, Pallas kernels, embed(): pl.pallas_call(functools.partial(embed_kernel, shard_rows), out_shape=(ja...  61.4 us
    pallas_call x2, Pallas kernels, collect_keys(): pl.pallas_call(functools.partial(collect_kernel, slabs), out_shape=jax.Sh...  51.8 us
    pallas_call x1, Pallas kernels, vocab_back(): pl.pallas_call(functools.partial(vocab_back_kernel, shard_rows, held), ou...  50.9 us
    pallas_call x1, Pallas kernels, gather_logits(): pl.pallas_call(functools.partial(logits_kernel, shard_rows), out_shape=(j...  49.7 us
    pallas_call x2, Pallas kernels, experts(): pl.pallas_call(experts_kernel, out_shape=(jax.ShapeDtypeStruct((own, widt...  46.3 us
    pallas_call x4, Pallas kernels, project(): pl.pallas_call(functools.partial(project_kernel, transposed, left is not...  42.8 us
    pallas_call x2, Pallas kernels, experts_back(): pl.pallas_call(experts_back_kernel, out_shape=(jax.ShapeDtypeStruct((own,...  40.4 us
  transfers between devices with their start and end apart: 14, of which 1 were waited for; matrix products, arithmetic and copies ran while one was open for 7% of the time, Pallas kernels for 52%

profile of v1, /device:TPU:0, one launch (start us, length us, event | category | flops | bytes accessed | tf_op | source)
XLA Modules:
  0.0 726.5 jit_solution(15232387735784307451)
XLA Ops:
  26.4 18.6 %shard_map.382 = f32[32,24,128]{2,1,0:T(8,128)S(1)} custom-call(f32[1,24,128]{2,1,0:T(8,128)S(1)} %fusion.11.source), custom_call_target="tpu_custom_call" | custom-call | bytes 37748736 | tf_op jit(solution)/shard_map/pallas_call | solution.py:123
  49.7 61.4 %shard_map.383 = (f32[128,768]{1,0:T(8,128)S(1)}, bf16[2,4,2,2,48,576]{5,4,3,2,1,0:T(8,128)(2,1)S(1)}, bf16[2,4,2,24,768]{4,3,2,1,0:T(8,128)(2,1)S(1)}) custom-call(bf16[1024,768]{1,0:T(8,128)(2,1)S(1)} %pad.23.table, f32[4,2,2,2,24,128]{5,4,3,2,1,0:T(8,128)S(1)} %bitcast.157, bf16[2,2,48,576]{3,2,1,0:T(8,128)(2,1)S(1)} %bitcast.179, ...), custom_call_target="tpu_custom_call" | custom-call | bytes 125829120 | tf_op jit(solution)/shard_map/pallas_call | solution.py:1307
  112.5 10.0 %shard_map.384 = (bf16[2,2,128,768]{3,2,1,0:T(8,128)(2,1)S(1)}, bf16[2,2,128,384]{3,2,1,0:T(8,128)(2,1)S(1)}, bf16[2,2,128,192]{3,2,1,0:T(8,128)(2,1)S(1)}) custom-call(bf16[128,768]{1,0:T(8,128)(2,1)S(1)} %multiply_convert_fusion.6.own_rows, bf16[768,576]{1,0:T(8,128)(2,1)S(1)} %bitcast.161), custom_call_target="tpu_custom_call" | custom-call | flops 452984832 | bytes 25165824 | tf_op jit(solution)/shard_map/pallas_call | solution.py:1814
  124.8 12.0 %shard_map.385 = (bf16[2,2,512,384]{3,2,1,0:T(8,128)(2,1)S(1)}, bf16[4,256,384]{2,1,0:T(8,128)(2,1)S(1)}, bf16[256,384]{1,0:T(8,128)(2,1)}) custom-call(bf16[512,384]{1,0:T(8,128)(2,1)S(1)} %bitcast.182), custom_call_target="tpu_custom_call" | custom-call | bytes 62914560 | tf_op jit(solution)/shard_map/pallas_call | solution.py:334
  149.5 10.5 %shard_map.386 = (f32[192,512]{1,0:T(8,128)S(1)}, bf16[512,192]{1,0:T(8,128)(2,1)S(1)}, f32[3,512]{1,0:T(4,128)S(1)}) custom-call(bf16[512,192]{1,0:T(8,128)(2,1)S(1)} %bitcast.209, bf16[2048,384]{1,0:T(8,128)(2,1)S(1)} %bitcast.199, bf16[1024,384]{1,0:T(8,128)(2,1)S(1)} %bitcast.203, s32[1,512]{1,0:T(1,128)S(1)} %bitcast.195, ...), custom_call_target="tpu_custom_call" | custom-call | flops 4026531840 | bytes 8388608 | tf_op jit(solution)/shard_map/pallas_call | solution.py:2003
  160.1 12.9 %shard_map.387 = f32[128,768]{1,0:T(8,128)S(1)} custom-call(bf16[2,2,128,192]{3,2,1,0:T(8,128)(2,1)S(1)} %bitcast.173, bf16[192,768]{1,0:T(8,128)(2,1)S(1)} %bitcast.165), custom_call_target="tpu_custom_call" | custom-call | flops 150994944 | bytes 25165824 | tf_op jit(solution)/shard_map/pallas_call | solution.py:1747
  174.2 23.5 %shard_map.388 = (f32[128,768]{1,0:T(8,128)}, bf16[2,2,128,768]{3,2,1,0:T(8,128)(2,1)}, f32[2,2,128,768]{3,2,1,0:T(8,128)}, bf16[2,2,128,768]{3,2,1,0:T(8,128)(2,1)}) custom-call(bf16[128,768]{1,0:T(8,128)(2,1)} %copy-done.64, s32[2,2,128,1]{3,2,1,0:T(8,128)} %copy.106.route, bf16[4,2,4,48,768]{4,3,2,1,0:T(8,128)(2,1)} %bitcast.238, ...), custom_call_target="tpu_custom_call" | custom-call | flops 2415919104 | bytes 56623104 | tf_op jit(solution)/shard_map/pallas_call | solution.py:1556
  209.2 20.5 %shard_map.390 = (bf16[2,2,512,384]{3,2,1,0:T(8,128)(2,1)S(1)}, bf16[4,256,384]{2,1,0:T(8,128)(2,1)S(1)}, bf16[256,384]{1,0:T(8,128)(2,1)}) custom-call(bf16[512,384]{1,0:T(8,128)(2,1)S(1)} %bitcast.183), custom_call_target="tpu_custom_call" | custom-call | bytes 62914560 | tf_op jit(solution)/shard_map/pallas_call | solution.py:334
  229.8 10.5 %shard_map.391 = (f32[192,512]{1,0:T(8,128)S(1)}, bf16[512,192]{1,0:T(8,128)(2,1)S(1)}, f32[3,512]{1,0:T(4,128)S(1)}) custom-call(bf16[512,192]{1,0:T(8,128)(2,1)S(1)} %bitcast.211, bf16[2048,384]{1,0:T(8,128)(2,1)S(1)} %bitcast.201, bf16[1024,384]{1,0:T(8,128)(2,1)S(1)} %bitcast.205, s32[1,512]{1,0:T(1,128)S(1)} %bitcast.196, ...), custom_call_target="tpu_custom_call" | custom-call | flops 4026531840 | bytes 8388608 | tf_op jit(solution)/shard_map/pallas_call | solution.py:2003
  240.4 12.3 %shard_map.392 = f32[128,768]{1,0:T(8,128)S(1)} custom-call(bf16[2,2,128,192]{3,2,1,0:T(8,128)(2,1)S(1)} %bitcast.174, bf16[192,768]{1,0:T(8,128)(2,1)S(1)} %bitcast.167), custom_call_target="tpu_custom_call" | custom-call | flops 150994944 | bytes 25165824 | tf_op jit(solution)/shard_map/pallas_call | solution.py:1747
  253.8 22.9 %shard_map.393 = (f32[128,768]{1,0:T(8,128)}, bf16[2,2,128,768]{3,2,1,0:T(8,128)(2,1)}, f32[2,2,128,768]{3,2,1,0:T(8,128)}, bf16[2,2,128,768]{3,2,1,0:T(8,128)(2,1)}) custom-call(bf16[128,768]{1,0:T(8,128)(2,1)} %copy-done.66, s32[2,2,128,1]{3,2,1,0:T(8,128)} %copy.107.route, bf16[4,2,4,48,768]{4,3,2,1,0:T(8,128)(2,1)} %bitcast.242, ...), custom_call_target="tpu_custom_call" | custom-call | flops 2415919104 | bytes 56623104 | tf_op jit(solution)/shard_map/pallas_call | solution.py:1556
  278.0 49.7 %shard_map.394 = (bf16[4,2,2,2,128,768]{5,4,3,2,1,0:T(8,128)(2,1)S(1)}, f32[4,2,2,2,1,128]{5,4,3,2,1,0:T(1,128)S(1)}, f32[1,256]{1,0:T(1,128)S(1)}) custom-call(bf16[128,768]{1,0:T(8,128)(2,1)S(1)} %multiply_convert_fusion.2.rows_in, bf16[1024,768]{1,0:T(8,128)(2,1)S(1)} %pad.23.table, f32[4,2,2,2,24,128]{5,4,3,2,1,0:T(8,128)S(1)} %bitcast.158, ...), custom_call_target="tpu_custom_call" | custom-call | bytes 113246208 | tf_op jit(solution)/shard_map/pallas_call | solution.py:968
  327.6 18.8 %shard_map.395 = f32[32,1,128]{2,1,0:T(1,128)S(1)} custom-call(f32[32,1,128]{2,1,0:T(1,128)S(1)} %bitcast.190), custom_call_target="tpu_custom_call" | custom-call | bytes 44040192 | tf_op jit(solution)/shard_map/pallas_call | solution.py:1888
  346.5 50.9 %shard_map.396 = (f32[128,768]{1,0:T(8,128)S(1)}, f32[1024,768]{1,0:T(8,128)S(1)}) custom-call(bf16[4,2,2,2,128,768]{5,4,3,2,1,0:T(8,128)(2,1)S(1)} %get-tuple-element.115.rows_all, bf16[1024,768]{1,0:T(8,128)(2,1)S(1)} %pad.23.table, f32[4,2,2,2,24,128]{5,4,3,2,1,0:T(8,128)S(1)} %bitcast.159, f32[4,2,2,2,1,128]{5,4,3,2,1,0:T(1,128)S(1)} %bitcast.188, ...), custom_call_target="tpu_custom_call" | custom-call | bytes 150994944 | tf_op jit(solution)/shard_map/pallas_call | solution.py:1382
  400.3 20.3 %shard_map.397 = (f32[128,768]{1,0:T(8,128)}, bf16[8,2,4,48,768]{4,3,2,1,0:T(8,128)(2,1)}) custom-call(bf16[128,768]{1,0:T(8,128)(2,1)} %multiply_convert_fusion.1.own_rows, s32[2,2,128,1]{3,2,1,0:T(8,128)} %copy.107.route, bf16[4,2,4,48,768]{4,3,2,1,0:T(8,128)(2,1)} %bitcast.243, bf16[4,2,4,48,768]{4,3,2,1,0:T(8,128)(2,1)} %bitcast.245, ...), custom_call_target="tpu_custom_call" | custom-call | flops 4831838208 | bytes 56623104 | tf_op jit(solution)/shard_map/pallas_call | solution.py:1668
  423.3 9.5 %shard_map.398 = (bf16[2,2,128,768]{3,2,1,0:T(8,128)(2,1)}, bf16[2,2,128,192]{3,2,1,0:T(8,128)(2,1)S(1)}, bf16[2,4,24,768]{3,2,1,0:T(8,128)(2,1)S(1)}) custom-call(bf16[128,768]{1,0:T(8,128)(2,1)S(1)} %get-tuple-element.198.own_rows, bf16[192,768]{1,0:T(8,128)(2,1)S(1)} %bitcast.168, bf16[512,192]{1,0:T(8,128)(2,1)S(1)} %copy-done.15), custom_call_target="tpu_custom_call" | custom-call | flops 150994944 | bytes 25165824 | tf_op jit(solution)/shard_map/pallas_call | solution.py:1814
  433.6 15.0 %shard_map.399 = (bf16[512,192]{1,0:T(8,128)(2,1)S(1)}, bf16[2048,384]{1,0:T(8,128)(2,1)S(1)}, bf16[1024,384]{1,0:T(8,128)(2,1)S(1)}) custom-call(bf16[512,192]{1,0:T(8,128)(2,1)S(1)} %bitcast.212, bf16[2048,384]{1,0:T(8,128)(2,1)S(1)} %bitcast.202, bf16[1024,384]{1,0:T(8,128)(2,1)S(1)} %bitcast.206, s32[1,512]{1,0:T(1,128)S(1)} %bitcast.197, ...), custom_call_target="tpu_custom_call" | custom-call | flops 10066329600 | bytes 12582912 | tf_op jit(solution)/shard_map/pallas_call | solution.py:2110
  448.6 20.8 %shard_map.400 = bf16[512,576]{1,0:T(8,128)(2,1)S(1)} custom-call(bf16[2,2,512,384]{3,2,1,0:T(8,128)(2,1)S(1)} %bitcast.172, bf16[4,256,384]{2,1,0:T(8,128)(2,1)S(1)} %bitcast.181, bf16[512,192]{1,0:T(8,128)(2,1)S(1)} %get-tuple-element.127.query_grad), custom_call_target="tpu_custom_call" | custom-call | bytes 62914560 | tf_op jit(solution)/shard_map/pallas_call | solution.py:496
  484.2 20.1 %shard_map.402 = (f32[128,768]{1,0:T(8,128)}, bf16[8,2,4,48,768]{4,3,2,1,0:T(8,128)(2,1)}) custom-call(bf16[128,768]{1,0:T(8,128)(2,1)} %multiply_convert_fusion.own_rows, s32[2,2,128,1]{3,2,1,0:T(8,128)} %copy.106.route, bf16[4,2,4,48,768]{4,3,2,1,0:T(8,128)(2,1)} %bitcast.239, bf16[4,2,4,48,768]{4,3,2,1,0:T(8,128)(2,1)} %bitcast.241, ...), custom_call_target="tpu_custom_call" | custom-call | flops 4831838208 | bytes 56623104 | tf_op jit(solution)/shard_map/pallas_call | solution.py:1668
  506.9 10.6 %shard_map.403 = (bf16[2,2,128,768]{3,2,1,0:T(8,128)(2,1)}, bf16[2,2,128,192]{3,2,1,0:T(8,128)(2,1)S(1)}, bf16[2,4,24,768]{3,2,1,0:T(8,128)(2,1)S(1)}) custom-call(bf16[128,768]{1,0:T(8,128)(2,1)S(1)} %get-tuple-element.194.own_rows, bf16[192,768]{1,0:T(8,128)(2,1)S(1)} %bitcast.166, bf16[512,192]{1,0:T(8,128)(2,1)S(1)} %copy-done.13), custom_call_target="tpu_custom_call" | custom-call | flops 150994944 | bytes 25165824 | tf_op jit(solution)/shard_map/pallas_call | solution.py:1814
  518.3 15.2 %shard_map.404 = (bf16[512,192]{1,0:T(8,128)(2,1)S(1)}, bf16[2048,384]{1,0:T(8,128)(2,1)S(1)}, bf16[1024,384]{1,0:T(8,128)(2,1)S(1)}) custom-call(bf16[512,192]{1,0:T(8,128)(2,1)S(1)} %bitcast.210, bf16[2048,384]{1,0:T(8,128)(2,1)S(1)} %bitcast.200, bf16[1024,384]{1,0:T(8,128)(2,1)S(1)} %bitcast.204, s32[1,512]{1,0:T(1,128)S(1)} %bitcast.198, ...), custom_call_target="tpu_custom_call" | custom-call | flops 10066329600 | bytes 12582912 | tf_op jit(solution)/shard_map/pallas_call | solution.py:2110
  533.5 31.0 %shard_map.405 = bf16[512,576]{1,0:T(8,128)(2,1)S(1)} custom-call(bf16[2,2,512,384]{3,2,1,0:T(8,128)(2,1)S(1)} %bitcast.171, bf16[4,256,384]{2,1,0:T(8,128)(2,1)S(1)} %bitcast.180, bf16[512,192]{1,0:T(8,128)(2,1)S(1)} %get-tuple-element.141.query_grad), custom_call_target="tpu_custom_call" | custom-call | bytes 62914560 | tf_op jit(solution)/shard_map/pallas_call | solution.py:496
  580.9 71.1 %shard_map.407 = (f32[1024,768]{1,0:T(8,128)S(1)}, f32[16,128]{1,0:T(8,128)S(1)}, f32[1,768]{1,0:T(1,128)S(1)}, f32[2,48,576]{2,1,0:T(8,128)S(1)}, f32[2,48,576]...) custom-call(bf16[128,768]{1,0:T(8,128)(2,1)S(1)} %fusion.9.rows_in, ...), custom_call_target="tpu_custom_call" | custom-call | bytes 125829120 | tf_op jit(solution)/shard_map/pallas_call | solution.py:1043
  683.2 9.8 %shard_map.408 = f32[32,8,128]{2,1,0:T(8,128)S(1)} custom-call(f32[1,8,128]{2,1,0:T(8,128)S(1)} %pad_bitcast_fusion.source), custom_call_target="tpu_custom_call" | custom-call | bytes 37748736 | tf_op jit(solution)/shard_map/pallas_call | solution.py:123
  (377 shorter events, 145.1 us)
Async XLA Ops:
  7.2 166.9 %all-gather.9.cloned.1.call-start = ((), (), s32[]{:S(2)}) async-start(), calls=%async_computation.6 | async-start | bytes 2654208 | tf_op jit(solution)/shard_map/all_gather | solution.py:2248
  12.8 32.2 %collective-permute-start = (bf16[2,24,768]{2,1,0:T(8,128)(2,1)S(1)}, bf16[2,24,768]{2,1,0:T(8,128)(2,1)S(1)}, u32[]{:S(2)}, u32[]{:S(2)}) collective-permute-start(bf16[2,24,768]{2,1,0:T(8,128)(2,1)S(1)} %slice.208), channel_id=1, source_target_pairs={{0,0},{1,2},{2,8},{3,10},{4,16},{5,18},{6,24},{7,26},{8,1},{9,3},{... | collective-permute-start | bytes 221192 | tf_op jit(solution)/shard_map/ppermute | solution.py:2225
  15.8 29.3 %all-to-all-start = ((bf16[4,2,24,576]{3,2,1,0:T(8,128)(2,1)}), bf16[4,2,24,576]{3,2,1,0:T(8,128)(2,1)S(1)}, u32[]{:S(2)}, u32[]{:S(2)}) async-start(bf16[4,2,24,576]{3,2,1,0:T(8,128)(2,1)} %reshape.483), calls=%async_computation | async-start | bytes 491520 | tf_op jit(solution)/shard_map/all_to_all | solution.py:2224
  24.1 150.0 %all-gather.11.cloned.1.call-start = ((), (), s32[]{:S(2)}) async-start(), calls=%async_computation.7 | async-start | bytes 2654208 | tf_op jit(solution)/shard_map/all_gather | solution.py:2250
  24.2 20.9 %collective-permute-start.1 = (bf16[4,48,768]{2,1,0:T(8,128)(2,1)S(1)}, bf16[4,48,768]{2,1,0:T(8,128)(2,1)S(1)}, u32[]{:S(2)}, u32[]{:S(2)}) collective-permute-start(bf16[4,48,768]{2,1,0:T(8,128)(2,1)S(1)} %bitcast.217), channel_id=1, source_target_pairs={{0,4},{4,0},{1,5},{5,1},{2,6},{6,2},{3,7},{7,3},{8,12},{12,8},{9,1... | collective-permute-start | bytes 884744 | tf_op jit(solution)/shard_map/ppermute | solution.py:2237
  45.8 207.9 %all-gather.13.cloned.1.call-start = ((), (), s32[]{:S(2)}) async-start(), calls=%async_computation.8 | async-start | bytes 2654208 | tf_op jit(solution)/shard_map/all_gather | solution.py:2248
  123.3 15.6 %copy-start.91 = (s32[16]{0:T(128)S(1)}, s32[16]{0:T(128)}, u32[]{:S(2)}) copy-start(s32[16]{0:T(128)} %param.26) | copy-start | bytes 196
  123.3 15.9 %copy-start.82 = (s32[4096]{0:T(1024)S(1)}, s32[4096]{0:T(1024)}, u32[]{:S(2)}) copy-start(s32[4096]{0:T(1024)} %param.25) | copy-start | bytes 49156
  123.3 15.5 %collective-permute-start.2 = (bf16[4,48,768]{2,1,0:T(8,128)(2,1)S(1)}, bf16[4,48,768]{2,1,0:T(8,128)(2,1)}, u32[]{:S(2)}, u32[]{:S(2)}) collective-permute-start(bf16[4,48,768]{2,1,0:T(8,128)(2,1)S(1)} %bitcast.216), channel_id=1, source_target_pairs={{0,4},{4,0},{1,5},{5,1},{2,6},{6,2},{3,7},{7,3},{8,12},{12,8},{9,1... | collective-permute-start | bytes 884744 | tf_op jit(solution)/shard_map/ppermute | solution.py:2237
  138.9 114.9 %all-gather.15.cloned.1.call-start = ((), (), s32[]{:S(2)}) async-start(), calls=%async_computation.9 | async-start | bytes 2654208 | tf_op jit(solution)/shard_map/all_gather | solution.py:2250
  146.0 524.9 %reduce-scatter.5.cloned.1.call-start = ((), (), s32[]{:S(2)}) async-start(), calls=%async_computation.5 | async-start | bytes 5308416 | tf_op jit(solution)/shard_map/reduce_scatter | solution.py:2380
  174.1 23.5 %copy-start.50 = (f32[128,768]{1,0:T(8,128)S(1)}, f32[128,768]{1,0:T(8,128)}, u32[]{:S(2)}) copy-start(f32[128,768]{1,0:T(8,128)} %copy-done.49) | copy-start | bytes 1179652
  199.0 53.7 %copy-start.52 = (f32[128,768]{1,0:T(8,128)}, f32[128,768]{1,0:T(8,128)S(1)}, u32[]{:S(2)}) copy-start(f32[128,768]{1,0:T(8,128)S(1)} %get-tuple-element.209) | copy-start | bytes 1179652
  209.2 31.1 %copy-start.42 = (bf16[2,2,128,192]{3,2,1,0:T(8,128)(2,1)}, bf16[2,2,128,192]{3,2,1,0:T(8,128)(2,1)S(1)}, u32[]{:S(2)}) copy-start(bf16[2,2,128,192]{3,2,1,0:T(8,128)(2,1)S(1)} %get-tuple-element.107) | copy-start | bytes 589828
  253.8 22.9 %copy-start.55 = (f32[128,768]{1,0:T(8,128)S(1)}, f32[128,768]{1,0:T(8,128)}, u32[]{:S(2)}) copy-start(f32[128,768]{1,0:T(8,128)} %copy-done.54) | copy-start | bytes 1179652
  346.4 52.8 %copy-start.69 = (f32[128,768]{1,0:T(8,128)S(1)}, f32[128,768]{1,0:T(8,128)}, u32[]{:S(2)}) copy-start(f32[128,768]{1,0:T(8,128)} %get-tuple-element.114) | copy-start | bytes 1179652
  470.2 206.3 %reduce-scatter.3.cloned.1.call-start = ((), (), s32[]{:S(2)}) async-start(), calls=%async_computation.4 | async-start | bytes 5308416 | tf_op jit(solution)/shard_map/reduce_scatter | solution.py:2380
  484.2 20.1 %copy-start.51 = (f32[128,768]{1,0:T(8,128)S(1)}, f32[128,768]{1,0:T(8,128)}, u32[]{:S(2)}) copy-start(f32[128,768]{1,0:T(8,128)} %copy-done.49) | copy-start | bytes 1179652
  504.3 14.0 %copy-start.36 = (bf16[4,256,384]{2,1,0:T(8,128)(2,1)S(1)}, bf16[4,256,384]{2,1,0:T(8,128)(2,1)}, u32[]{:S(2)}) copy-start(bf16[4,256,384]{2,1,0:T(8,128)(2,1)} %copy-done.34) | copy-start | bytes 2359300
  654.6 11.6 %all-to-all-start.1 = ((f32[4,2,24,576]{3,2,1,0:T(8,128)}), f32[4,2,24,576]{3,2,1,0:T(8,128)S(1)}, u32[]{:S(2)}, u32[]{:S(2)}) async-start(f32[4,2,24,576]{3,2,1,0:T(8,128)} %bitcast.76), calls=%async_computation.3 | async-start | bytes 983040 | tf_op jit(solution)/shard_map/all_to_all | solution.py:2428
  660.4 43.0 %collective-permute-start.3 = (f32[2,24,768]{2,1,0:T(8,128)}, f32[2,24,768]{2,1,0:T(8,128)}, u32[]{:S(2)}, u32[]{:S(2)}) collective-permute-start(f32[2,24,768]{2,1,0:T(8,128)} %pad_maximum_fusion.2), channel_id=1, source_target_pairs={{0,0},{2,1},{8,2},{10,3},{16,4},{18,5},{24,6},{26,7},{1,8},{3,9},{... | collective-permute-start | bytes 442376 | tf_op jit(solution)/shard_map/ppermute | solution.py:2432
  668.6 27.9 %copy-start.5 = (f32[1024,768]{1,0:T(8,128)S(1)}, f32[1024,768]{1,0:T(8,128)}, u32[]{:S(2)}) copy-start(f32[1024,768]{1,0:T(8,128)} %copy-done.4) | copy-start | bytes 9437188
  671.9 35.3 %collective-permute-start.5 = (bf16[4,48,768]{2,1,0:T(8,128)(2,1)S(1)}, bf16[4,48,768]{2,1,0:T(8,128)(2,1)}, u32[]{:S(2)}, u32[]{:S(2)}) collective-permute-start(bf16[4,48,768]{2,1,0:T(8,128)(2,1)S(1)} %dynamic-slice_bitcast_fusion), channel_id=1, source_target_pairs={{0,4},{4,0},{1,5},{5,1},{2,6},{6,2},{3,7},{7,3},{8,12},{12,8},{9,1... | collective-permute-start | bytes 884744 | tf_op jit(solution)/shard_map/ppermute | solution.py:2411
  695.5 12.9 %collective-permute-start.4 = (bf16[4,48,768]{2,1,0:T(8,128)(2,1)S(1)}, bf16[4,48,768]{2,1,0:T(8,128)(2,1)S(1)}, u32[]{:S(2)}, u32[]{:S(2)}) collective-permute-start(bf16[4,48,768]{2,1,0:T(8,128)(2,1)S(1)} %dynamic-slice_bitcast_fusion.1), channel_id=1, source_target_pairs={{0,4},{4,0},{1,5},{5,1},{2,6},{6,2},{3,7},{7,3},{8,12},{12,8},{9,1... | collective-permute-start | bytes 884744 | tf_op jit(solution)/shard_map/ppermute | solution.py:2411
  (82 other events, 404.1 us)
Sparse Core Ops, SparseCore 0:
  12.5 42.9 all-gather.8
  57.7 40.0 all-gather.10
  139.0 44.7 all-gather.12
  185.3 30.7 all-gather.14
  470.3 58.1 reduce-scatter.4
  564.7 88.5 reduce-scatter.2
